TPU v7x, 128 devices: a whole 4x4x4 slice. The times are simulated.
128 devices in a mesh: section: 16 (over x, z), expert: 8 (over y, core).
Axes of the slice: x: 4, y: 4, z: 4, core: 2. Of those that a mesh axis runs over, the one named last changes fastest.
Arguments:
- tokens: bfloat16 [2048, 4096], P(('section', 'expert')), may hold values from -6 to 6
- routes: int32 [2048, 2], P(('section', 'expert')), may hold values from 0 to 7, all different within a row; in each aligned block of 16 rows (0 to 15, 16 to 31, ...) at most 8 rows name the same one
- router_weight: bfloat16 [4096, 8], replicated, may hold values from -0.09375 to 0.09375
- gate_weight: bfloat16 [8, 4096, 14336], P('expert', None, 'section'), may hold values from -0.09375 to 0.09375
- up_weight: bfloat16 [8, 4096, 14336], P('expert', None, 'section'), may hold values from -0.09375 to 0.09375
- down_weight: bfloat16 [8, 14336, 4096], P('expert', 'section'), may hold values from -0.046875 to 0.046875
Outputs:
- mixed: bfloat16 [2048, 4096], P(('section', 'expert'))
Inputs may be any that keep to these rules, and one draw needn't show every extreme that they name: `routes`: each token names two different experts; the 16 tokens of one device name one expert at most 8 times, and in every draw some device's tokens name some expert exactly 8 times.
All inputs are finite; a program needn't handle non-finite values.
Results may differ from a plain program's by a relative error of at most 0.024.
Values may be sent and summed in bfloat16 or wider, within the bound.
A program may use at most 128 MiB of HBM per device.

v0:
```python
import jax
import jax.numpy as jnp
from jax import lax
from jax.sharding import PartitionSpec as P


def from_behind(block, axis, distance):
    devices = range(lax.axis_size(axis))
    route = [((i - distance) % len(devices), i) for i in devices]
    return lax.ppermute(block, axis, route)


def shards(tokens, routes, router_weight, gate_weight, up_weight, down_weight):
    tok_rows = tokens.shape[0]
    width_model = tokens.shape[1]
    experts = router_weight.shape[1]
    capacity = tok_rows // 2
    buffer_rows = experts * capacity
    logits = jnp.dot(tokens, router_weight, preferred_element_type=jnp.float32)
    chosen = jnp.take_along_axis(logits, routes, axis=1)
    first_gate = jax.nn.sigmoid(chosen[:, 0] - chosen[:, 1])
    gate_pair = jnp.stack([first_gate, 1.0 - first_gate], axis=1)
    onehot = (routes[:, :, None] == jnp.arange(experts, dtype=jnp.int32)[None, None, :]).astype(
        jnp.int32
    )
    flat_hot = onehot.reshape(tok_rows * 2, experts)
    earlier = jnp.cumsum(flat_hot, axis=0) - flat_hot
    slot_index = jnp.sum(earlier * flat_hot, axis=1).reshape(tok_rows, 2)
    target = routes * capacity + slot_index
    placing = (
        target[:, :, None] == jnp.arange(buffer_rows, dtype=jnp.int32)[None, None, :]
    ).astype(jnp.float32)
    dispatch = jnp.sum(placing, axis=1).astype(jnp.bfloat16)
    outgoing = jnp.dot(dispatch.T, tokens, preferred_element_type=jnp.float32).astype(jnp.bfloat16)
    outgoing = outgoing.reshape(experts, capacity, width_model)
    received = lax.all_to_all(outgoing, "expert", split_axis=0, concat_axis=0, tiled=True)
    arrived = received.reshape(-1, width_model)
    w_gate = gate_weight[0]
    w_up = up_weight[0]
    w_down = down_weight[0]

    def section_term(block_rows):
        gate_act = jnp.dot(block_rows, w_gate, preferred_element_type=jnp.float32)
        up_act = jnp.dot(block_rows, w_up, preferred_element_type=jnp.float32)
        hidden = (jax.nn.silu(gate_act) * up_act).astype(jnp.bfloat16)
        partial_sum = jnp.dot(hidden, w_down, preferred_element_type=jnp.float32).astype(
            jnp.bfloat16
        )
        partial_sum = lax.optimization_barrier(partial_sum)
        return partial_sum.astype(jnp.float32)

    sections = lax.axis_size("section")

    def pass_sums(running):
        return from_behind(running.astype(jnp.bfloat16), "section", 1).astype(running.dtype)

    def one_step(position, state_pair):
        rows_now, running = state_pair
        running = pass_sums(running + section_term(rows_now))
        rows_now = from_behind(rows_now, "section", 1)
        return (rows_now, running)

    start_sum = jnp.zeros(arrived.shape, jnp.float32)
    rows_now, running = lax.fori_loop(0, sections - 1, one_step, (arrived, start_sum))
    summed = pass_sums(running + section_term(rows_now))
    expert_out = summed.astype(jnp.bfloat16).reshape(experts, capacity, width_model)
    returned = lax.all_to_all(expert_out, "expert", split_axis=0, concat_axis=0, tiled=True)
    combine = jnp.sum(gate_pair[:, :, None] * placing, axis=1)
    mixed = jnp.dot(
        combine,
        returned.reshape(buffer_rows, width_model).astype(jnp.float32),
        precision=lax.Precision.HIGHEST,
    )
    return mixed.astype(jnp.bfloat16)


def solution(mesh):
    in_specs = (
        P(("section", "expert"), None),
        P(("section", "expert"), None),
        P(),
        P("expert", None, "section"),
        P("expert", None, "section"),
        P("expert", "section", None),
    )
    out_specs = P(("section", "expert"), None)
    return jax.shard_map(shards, mesh=mesh, in_specs=in_specs, out_specs=out_specs, check_vma=False)
```

profile of v0, /device:TPU:0, one launch (start us, length us, event | category | flops | bytes accessed | tf_op | source)
XLA Modules:
  0.0 583.4 jit_solution(871160214911377782)
XLA Ops:
  5.4 4.5 all-to-all-start
  9.9 10.3 %all-to-all-done = bf16[8,8,4096]{2,1,0:T(8,128)(2,1)S(1)} async-done(((bf16[8,8,4096]{2,1,0:T(8,128)(2,1)}), bf16[8,8,4096]{2,1,0:T(8,128)(2,1)S(1)}, u32[]{:S(2)}, u32[]{:S(2)}) %all-to-all-start) | async-done | bytes 524320 | tf_op jit(solution)/shard_map/all_to_all | solution.py:36
  20.3 521.8 %while.13 = (s32[]{:T(128)}, bf16[64,4096]{1,0:T(8,128)(2,1)S(1)}, f32[64,4096]{1,0:T(8,128)S(1)}, bf16[4096,896]{1,0:T(8,128)(2,1)}, bf16[4096,896]{1,0:T(8,128...) while((s32[]{:T(128)}, bf16[64,4096]{1,0:T(8,128)(2,1)S(1)}, ...), condition=%wide.region_5.6_spmd.clone, body=%wide.region_4.5_spmd.clone.sunk | while | flops 1411203072 | bytes 32964780 | solution.py:64
  20.3 4.3 fusion.52
  24.6 7.9 %convolution_convert_fusion.5 = bf16[64,4096]{1,0:T(8,128)(2,1)S(1)} fusion(bf16[896,4096]{1,0:T(8,128)(2,1)} %get-tuple-element.135, bf16[64,4096]{1,0:T(8,128)(2,1)S(1)} %copy.60, bf16[4096,896]{1,0:T(8,128)(2,1)} %get-tuple-element.134, f32[64,896]{1,0:T(8,128)S(1)} %fusion.52), kind=kOutput, calls=%fused_computation.1.clone.1 | convolution fusion | flops 940130304 | bytes 15958016 | tf_op jit(solution)/shard_map/while/body/eval_jaxpr/dot_general | solution.py:46
  36.6 15.2 %collective-permute-done.1 = bf16[64,4096]{1,0:T(8,128)(2,1)S(1)} collective-permute-done((bf16[64,4096]{1,0:T(8,128)(2,1)S(1)}, bf16[64,4096]{1,0:T(8,128)(2,1)S(1)}, u32[]{:S(2)}, u32[]{:S(2)}) %collective-permute-start.1) | collective-permute-done | bytes 524320 | tf_op jit(solution)/shard_map/while/body/eval_jaxpr/ppermute | solution.py:10
  51.8 10.1 %collective-permute-done = bf16[64,4096]{1,0:T(8,128)(2,1)S(1)} collective-permute-done((bf16[64,4096]{1,0:T(8,128)(2,1)S(1)}, bf16[64,4096]{1,0:T(8,128)(2,1)S(1)}, u32[]{:S(2)}, u32[]{:S(2)}) %collective-permute-start) | collective-permute-done | bytes 524320 | tf_op jit(solution)/shard_map/while/body/eval_jaxpr/ppermute | solution.py:10
  66.3 7.9 %convolution_convert_fusion.5 = bf16[64,4096]{1,0:T(8,128)(2,1)S(1)} fusion(bf16[896,4096]{1,0:T(8,128)(2,1)} %get-tuple-element.135, bf16[64,4096]{1,0:T(8,128)(2,1)S(1)} %copy.60, bf16[4096,896]{1,0:T(8,128)(2,1)} %get-tuple-element.134, f32[64,896]{1,0:T(8,128)S(1)} %fusion.52), kind=kOutput, calls=%fused_computation.1.clone.1 | convolution fusion | flops 940130304 | bytes 15958016 | tf_op jit(solution)/shard_map/while/body/eval_jaxpr/dot_general | solution.py:46
  74.5 18.1 %collective-permute-done.1 = bf16[64,4096]{1,0:T(8,128)(2,1)S(1)} collective-permute-done((bf16[64,4096]{1,0:T(8,128)(2,1)S(1)}, bf16[64,4096]{1,0:T(8,128)(2,1)S(1)}, u32[]{:S(2)}, u32[]{:S(2)}) %collective-permute-start.1) | collective-permute-done | bytes 524320 | tf_op jit(solution)/shard_map/while/body/eval_jaxpr/ppermute | solution.py:10
  92.7 9.2 %collective-permute-done = bf16[64,4096]{1,0:T(8,128)(2,1)S(1)} collective-permute-done((bf16[64,4096]{1,0:T(8,128)(2,1)S(1)}, bf16[64,4096]{1,0:T(8,128)(2,1)S(1)}, u32[]{:S(2)}, u32[]{:S(2)}) %collective-permute-start) | collective-permute-done | bytes 524320 | tf_op jit(solution)/shard_map/while/body/eval_jaxpr/ppermute | solution.py:10
  101.9 4.3 fusion.52
  106.2 7.9 %convolution_convert_fusion.5 = bf16[64,4096]{1,0:T(8,128)(2,1)S(1)} fusion(bf16[896,4096]{1,0:T(8,128)(2,1)} %get-tuple-element.135, bf16[64,4096]{1,0:T(8,128)(2,1)S(1)} %copy.60, bf16[4096,896]{1,0:T(8,128)(2,1)} %get-tuple-element.134, f32[64,896]{1,0:T(8,128)S(1)} %fusion.52), kind=kOutput, calls=%fused_computation.1.clone.1 | convolution fusion | flops 940130304 | bytes 15958016 | tf_op jit(solution)/shard_map/while/body/eval_jaxpr/dot_general | solution.py:46
  114.4 18.1 %collective-permute-done.1 = bf16[64,4096]{1,0:T(8,128)(2,1)S(1)} collective-permute-done((bf16[64,4096]{1,0:T(8,128)(2,1)S(1)}, bf16[64,4096]{1,0:T(8,128)(2,1)S(1)}, u32[]{:S(2)}, u32[]{:S(2)}) %collective-permute-start.1) | collective-permute-done | bytes 524320 | tf_op jit(solution)/shard_map/while/body/eval_jaxpr/ppermute | solution.py:10
  132.6 8.3 %collective-permute-done = bf16[64,4096]{1,0:T(8,128)(2,1)S(1)} collective-permute-done((bf16[64,4096]{1,0:T(8,128)(2,1)S(1)}, bf16[64,4096]{1,0:T(8,128)(2,1)S(1)}, u32[]{:S(2)}, u32[]{:S(2)}) %collective-permute-start) | collective-permute-done | bytes 524320 | tf_op jit(solution)/shard_map/while/body/eval_jaxpr/ppermute | solution.py:10
  140.9 4.3 fusion.52
  145.2 7.9 %convolution_convert_fusion.5 = bf16[64,4096]{1,0:T(8,128)(2,1)S(1)} fusion(bf16[896,4096]{1,0:T(8,128)(2,1)} %get-tuple-element.135, bf16[64,4096]{1,0:T(8,128)(2,1)S(1)} %copy.60, bf16[4096,896]{1,0:T(8,128)(2,1)} %get-tuple-element.134, f32[64,896]{1,0:T(8,128)S(1)} %fusion.52), kind=kOutput, calls=%fused_computation.1.clone.1 | convolution fusion | flops 940130304 | bytes 15958016 | tf_op jit(solution)/shard_map/while/body/eval_jaxpr/dot_general | solution.py:46
  153.4 18.1 %collective-permute-done.1 = bf16[64,4096]{1,0:T(8,128)(2,1)S(1)} collective-permute-done((bf16[64,4096]{1,0:T(8,128)(2,1)S(1)}, bf16[64,4096]{1,0:T(8,128)(2,1)S(1)}, u32[]{:S(2)}, u32[]{:S(2)}) %collective-permute-start.1) | collective-permute-done | bytes 524320 | tf_op jit(solution)/shard_map/while/body/eval_jaxpr/ppermute | solution.py:10
  171.6 7.3 %collective-permute-done = bf16[64,4096]{1,0:T(8,128)(2,1)S(1)} collective-permute-done((bf16[64,4096]{1,0:T(8,128)(2,1)S(1)}, bf16[64,4096]{1,0:T(8,128)(2,1)S(1)}, u32[]{:S(2)}, u32[]{:S(2)}) %collective-permute-start) | collective-permute-done | bytes 524320 | tf_op jit(solution)/shard_map/while/body/eval_jaxpr/ppermute | solution.py:10
  179.0 4.3 fusion.52
  183.3 7.9 %convolution_convert_fusion.5 = bf16[64,4096]{1,0:T(8,128)(2,1)S(1)} fusion(bf16[896,4096]{1,0:T(8,128)(2,1)} %get-tuple-element.135, bf16[64,4096]{1,0:T(8,128)(2,1)S(1)} %copy.60, bf16[4096,896]{1,0:T(8,128)(2,1)} %get-tuple-element.134, f32[64,896]{1,0:T(8,128)S(1)} %fusion.52), kind=kOutput, calls=%fused_computation.1.clone.1 | convolution fusion | flops 940130304 | bytes 15958016 | tf_op jit(solution)/shard_map/while/body/eval_jaxpr/dot_general | solution.py:46
  191.5 18.1 %collective-permute-done.1 = bf16[64,4096]{1,0:T(8,128)(2,1)S(1)} collective-permute-done((bf16[64,4096]{1,0:T(8,128)(2,1)S(1)}, bf16[64,4096]{1,0:T(8,128)(2,1)S(1)}, u32[]{:S(2)}, u32[]{:S(2)}) %collective-permute-start.1) | collective-permute-done | bytes 524320 | tf_op jit(solution)/shard_map/while/body/eval_jaxpr/ppermute | solution.py:10
  209.7 6.4 %collective-permute-done = bf16[64,4096]{1,0:T(8,128)(2,1)S(1)} collective-permute-done((bf16[64,4096]{1,0:T(8,128)(2,1)S(1)}, bf16[64,4096]{1,0:T(8,128)(2,1)S(1)}, u32[]{:S(2)}, u32[]{:S(2)}) %collective-permute-start) | collective-permute-done | bytes 524320 | tf_op jit(solution)/shard_map/while/body/eval_jaxpr/ppermute | solution.py:10
  216.1 4.3 fusion.52
  220.4 7.9 %convolution_convert_fusion.5 = bf16[64,4096]{1,0:T(8,128)(2,1)S(1)} fusion(bf16[896,4096]{1,0:T(8,128)(2,1)} %get-tuple-element.135, bf16[64,4096]{1,0:T(8,128)(2,1)S(1)} %copy.60, bf16[4096,896]{1,0:T(8,128)(2,1)} %get-tuple-element.134, f32[64,896]{1,0:T(8,128)S(1)} %fusion.52), kind=kOutput, calls=%fused_computation.1.clone.1 | convolution fusion | flops 940130304 | bytes 15958016 | tf_op jit(solution)/shard_map/while/body/eval_jaxpr/dot_general | solution.py:46
  228.7 18.0 %collective-permute-done.1 = bf16[64,4096]{1,0:T(8,128)(2,1)S(1)} collective-permute-done((bf16[64,4096]{1,0:T(8,128)(2,1)S(1)}, bf16[64,4096]{1,0:T(8,128)(2,1)S(1)}, u32[]{:S(2)}, u32[]{:S(2)}) %collective-permute-start.1) | collective-permute-done | bytes 524320 | tf_op jit(solution)/shard_map/while/body/eval_jaxpr/ppermute | solution.py:10
  246.8 5.5 collective-permute-done
  252.4 4.3 fusion.52
  256.7 7.9 %convolution_convert_fusion.5 = bf16[64,4096]{1,0:T(8,128)(2,1)S(1)} fusion(bf16[896,4096]{1,0:T(8,128)(2,1)} %get-tuple-element.135, bf16[64,4096]{1,0:T(8,128)(2,1)S(1)} %copy.60, bf16[4096,896]{1,0:T(8,128)(2,1)} %get-tuple-element.134, f32[64,896]{1,0:T(8,128)S(1)} %fusion.52), kind=kOutput, calls=%fused_computation.1.clone.1 | convolution fusion | flops 940130304 | bytes 15958016 | tf_op jit(solution)/shard_map/while/body/eval_jaxpr/dot_general | solution.py:46
  264.9 17.1 %collective-permute-done.1 = bf16[64,4096]{1,0:T(8,128)(2,1)S(1)} collective-permute-done((bf16[64,4096]{1,0:T(8,128)(2,1)S(1)}, bf16[64,4096]{1,0:T(8,128)(2,1)S(1)}, u32[]{:S(2)}, u32[]{:S(2)}) %collective-permute-start.1) | collective-permute-done | bytes 524320 | tf_op jit(solution)/shard_map/while/body/eval_jaxpr/ppermute | solution.py:10
  282.1 5.5 collective-permute-done
  287.7 4.3 fusion.52
  292.0 7.9 %convolution_convert_fusion.5 = bf16[64,4096]{1,0:T(8,128)(2,1)S(1)} fusion(bf16[896,4096]{1,0:T(8,128)(2,1)} %get-tuple-element.135, bf16[64,4096]{1,0:T(8,128)(2,1)S(1)} %copy.60, bf16[4096,896]{1,0:T(8,128)(2,1)} %get-tuple-element.134, f32[64,896]{1,0:T(8,128)S(1)} %fusion.52), kind=kOutput, calls=%fused_computation.1.clone.1 | convolution fusion | flops 940130304 | bytes 15958016 | tf_op jit(solution)/shard_map/while/body/eval_jaxpr/dot_general | solution.py:46
  300.2 16.2 %collective-permute-done.1 = bf16[64,4096]{1,0:T(8,128)(2,1)S(1)} collective-permute-done((bf16[64,4096]{1,0:T(8,128)(2,1)S(1)}, bf16[64,4096]{1,0:T(8,128)(2,1)S(1)}, u32[]{:S(2)}, u32[]{:S(2)}) %collective-permute-start.1) | collective-permute-done | bytes 524320 | tf_op jit(solution)/shard_map/while/body/eval_jaxpr/ppermute | solution.py:10
  316.4 5.5 collective-permute-done
  322.0 4.3 fusion.52
  326.4 7.9 %convolution_convert_fusion.5 = bf16[64,4096]{1,0:T(8,128)(2,1)S(1)} fusion(bf16[896,4096]{1,0:T(8,128)(2,1)} %get-tuple-element.135, bf16[64,4096]{1,0:T(8,128)(2,1)S(1)} %copy.60, bf16[4096,896]{1,0:T(8,128)(2,1)} %get-tuple-element.134, f32[64,896]{1,0:T(8,128)S(1)} %fusion.52), kind=kOutput, calls=%fused_computation.1.clone.1 | convolution fusion | flops 940130304 | bytes 15958016 | tf_op jit(solution)/shard_map/while/body/eval_jaxpr/dot_general | solution.py:46
  334.6 15.3 %collective-permute-done.1 = bf16[64,4096]{1,0:T(8,128)(2,1)S(1)} collective-permute-done((bf16[64,4096]{1,0:T(8,128)(2,1)S(1)}, bf16[64,4096]{1,0:T(8,128)(2,1)S(1)}, u32[]{:S(2)}, u32[]{:S(2)}) %collective-permute-start.1) | collective-permute-done | bytes 524320 | tf_op jit(solution)/shard_map/while/body/eval_jaxpr/ppermute | solution.py:10
  349.9 5.5 collective-permute-done
  355.5 4.3 fusion.52
  359.8 7.9 %convolution_convert_fusion.5 = bf16[64,4096]{1,0:T(8,128)(2,1)S(1)} fusion(bf16[896,4096]{1,0:T(8,128)(2,1)} %get-tuple-element.135, bf16[64,4096]{1,0:T(8,128)(2,1)S(1)} %copy.60, bf16[4096,896]{1,0:T(8,128)(2,1)} %get-tuple-element.134, f32[64,896]{1,0:T(8,128)S(1)} %fusion.52), kind=kOutput, calls=%fused_computation.1.clone.1 | convolution fusion | flops 940130304 | bytes 15958016 | tf_op jit(solution)/shard_map/while/body/eval_jaxpr/dot_general | solution.py:46
  368.0 14.3 %collective-permute-done.1 = bf16[64,4096]{1,0:T(8,128)(2,1)S(1)} collective-permute-done((bf16[64,4096]{1,0:T(8,128)(2,1)S(1)}, bf16[64,4096]{1,0:T(8,128)(2,1)S(1)}, u32[]{:S(2)}, u32[]{:S(2)}) %collective-permute-start.1) | collective-permute-done | bytes 524320 | tf_op jit(solution)/shard_map/while/body/eval_jaxpr/ppermute | solution.py:10
  382.4 5.5 collective-permute-done
  388.0 4.3 fusion.52
  392.3 7.9 %convolution_convert_fusion.5 = bf16[64,4096]{1,0:T(8,128)(2,1)S(1)} fusion(bf16[896,4096]{1,0:T(8,128)(2,1)} %get-tuple-element.135, bf16[64,4096]{1,0:T(8,128)(2,1)S(1)} %copy.60, bf16[4096,896]{1,0:T(8,128)(2,1)} %get-tuple-element.134, f32[64,896]{1,0:T(8,128)S(1)} %fusion.52), kind=kOutput, calls=%fused_computation.1.clone.1 | convolution fusion | flops 940130304 | bytes 15958016 | tf_op jit(solution)/shard_map/while/body/eval_jaxpr/dot_general | solution.py:46
  400.5 13.4 %collective-permute-done.1 = bf16[64,4096]{1,0:T(8,128)(2,1)S(1)} collective-permute-done((bf16[64,4096]{1,0:T(8,128)(2,1)S(1)}, bf16[64,4096]{1,0:T(8,128)(2,1)S(1)}, u32[]{:S(2)}, u32[]{:S(2)}) %collective-permute-start.1) | collective-permute-done | bytes 524320 | tf_op jit(solution)/shard_map/while/body/eval_jaxpr/ppermute | solution.py:10
  414.0 5.5 collective-permute-done
  419.6 4.3 fusion.52
  423.9 7.9 %convolution_convert_fusion.5 = bf16[64,4096]{1,0:T(8,128)(2,1)S(1)} fusion(bf16[896,4096]{1,0:T(8,128)(2,1)} %get-tuple-element.135, bf16[64,4096]{1,0:T(8,128)(2,1)S(1)} %copy.60, bf16[4096,896]{1,0:T(8,128)(2,1)} %get-tuple-element.134, f32[64,896]{1,0:T(8,128)S(1)} %fusion.52), kind=kOutput, calls=%fused_computation.1.clone.1 | convolution fusion | flops 940130304 | bytes 15958016 | tf_op jit(solution)/shard_map/while/body/eval_jaxpr/dot_general | solution.py:46
  432.1 12.5 %collective-permute-done.1 = bf16[64,4096]{1,0:T(8,128)(2,1)S(1)} collective-permute-done((bf16[64,4096]{1,0:T(8,128)(2,1)S(1)}, bf16[64,4096]{1,0:T(8,128)(2,1)S(1)}, u32[]{:S(2)}, u32[]{:S(2)}) %collective-permute-start.1) | collective-permute-done | bytes 524320 | tf_op jit(solution)/shard_map/while/body/eval_jaxpr/ppermute | solution.py:10
  444.7 5.5 collective-permute-done
  454.6 7.9 %convolution_convert_fusion.5 = bf16[64,4096]{1,0:T(8,128)(2,1)S(1)} fusion(bf16[896,4096]{1,0:T(8,128)(2,1)} %get-tuple-element.135, bf16[64,4096]{1,0:T(8,128)(2,1)S(1)} %copy.60, bf16[4096,896]{1,0:T(8,128)(2,1)} %get-tuple-element.134, f32[64,896]{1,0:T(8,128)S(1)} %fusion.52), kind=kOutput, calls=%fused_computation.1.clone.1 | convolution fusion | flops 940130304 | bytes 15958016 | tf_op jit(solution)/shard_map/while/body/eval_jaxpr/dot_general | solution.py:46
  462.8 12.4 %collective-permute-done.1 = bf16[64,4096]{1,0:T(8,128)(2,1)S(1)} collective-permute-done((bf16[64,4096]{1,0:T(8,128)(2,1)S(1)}, bf16[64,4096]{1,0:T(8,128)(2,1)S(1)}, u32[]{:S(2)}, u32[]{:S(2)}) %collective-permute-start.1) | collective-permute-done | bytes 524320 | tf_op jit(solution)/shard_map/while/body/eval_jaxpr/ppermute | solution.py:10
  475.3 5.5 collective-permute-done
  480.9 4.3 fusion.52
  485.2 7.9 %convolution_convert_fusion.5 = bf16[64,4096]{1,0:T(8,128)(2,1)S(1)} fusion(bf16[896,4096]{1,0:T(8,128)(2,1)} %get-tuple-element.135, bf16[64,4096]{1,0:T(8,128)(2,1)S(1)} %copy.60, bf16[4096,896]{1,0:T(8,128)(2,1)} %get-tuple-element.134, f32[64,896]{1,0:T(8,128)S(1)} %fusion.52), kind=kOutput, calls=%fused_computation.1.clone.1 | convolution fusion | flops 940130304 | bytes 15958016 | tf_op jit(solution)/shard_map/while/body/eval_jaxpr/dot_general | solution.py:46
  493.4 12.4 %collective-permute-done.1 = bf16[64,4096]{1,0:T(8,128)(2,1)S(1)} collective-permute-done((bf16[64,4096]{1,0:T(8,128)(2,1)S(1)}, bf16[64,4096]{1,0:T(8,128)(2,1)S(1)}, u32[]{:S(2)}, u32[]{:S(2)}) %collective-permute-start.1) | collective-permute-done | bytes 524320 | tf_op jit(solution)/shard_map/while/body/eval_jaxpr/ppermute | solution.py:10
  505.9 5.5 collective-permute-done
  511.5 4.3 fusion.52
  515.8 7.9 %convolution_convert_fusion.5 = bf16[64,4096]{1,0:T(8,128)(2,1)S(1)} fusion(bf16[896,4096]{1,0:T(8,128)(2,1)} %get-tuple-element.135, bf16[64,4096]{1,0:T(8,128)(2,1)S(1)} %copy.60, bf16[4096,896]{1,0:T(8,128)(2,1)} %get-tuple-element.134, f32[64,896]{1,0:T(8,128)S(1)} %fusion.52), kind=kOutput, calls=%fused_computation.1.clone.1 | convolution fusion | flops 940130304 | bytes 15958016 | tf_op jit(solution)/shard_map/while/body/eval_jaxpr/dot_general | solution.py:46
  524.0 12.4 %collective-permute-done.1 = bf16[64,4096]{1,0:T(8,128)(2,1)S(1)} collective-permute-done((bf16[64,4096]{1,0:T(8,128)(2,1)S(1)}, bf16[64,4096]{1,0:T(8,128)(2,1)S(1)}, u32[]{:S(2)}, u32[]{:S(2)}) %collective-permute-start.1) | collective-permute-done | bytes 524320 | tf_op jit(solution)/shard_map/while/body/eval_jaxpr/ppermute | solution.py:10
  536.5 5.5 collective-permute-done
  546.4 7.9 %convolution_convert_fusion.1 = bf16[64,4096]{1,0:T(8,128)(2,1)S(1)} fusion(bf16[64,4096]{1,0:T(8,128)(2,1)S(1)} %get-tuple-element.39, f32[64,896]{1,0:T(8,128)S(1)} %fusion.23, bf16[1,896,4096]{2,1,0:T(8,128)(2,1)} %bitcast.48, bf16[1,4096,896]{2,1,0:T(8,128)(2,1)} %bitcast.46), kind=kOutput, calls=%fused_computation.13 | convolution fusion | flops 940130304 | bytes 15958016 | tf_op jit(solution)/shard_map/dot_general | solution.py:46
  554.5 12.5 %collective-permute-done.2 = bf16[64,4096]{1,0:T(8,128)(2,1)S(1)} collective-permute-done((bf16[64,4096]{1,0:T(8,128)(2,1)S(1)}, bf16[64,4096]{1,0:T(8,128)(2,1)S(1)}, u32[]{:S(2)}, u32[]{:S(2)}) %collective-permute-start.2) | collective-permute-done | bytes 524320 | tf_op jit(solution)/shard_map/ppermute | solution.py:10
  566.9 15.5 %all_to_all.10 = bf16[8,8,4096]{2,1,0:T(8,128)(2,1)S(1)} all-to-all(bf16[8,8,4096]{2,1,0:T(8,128)(2,1)S(1)} %bitcast.50), channel_id=1, replica_groups=mesh['section'=16,'expert'=8] {'expert'}, dimensions={0} | all-to-all | bytes 1048576 | tf_op jit(solution)/shard_map/all_to_all | solution.py:67
  (106 shorter events, 28.9 us)
Async XLA Ops:
  0.0 1.7 copy-start
  0.0 3.5 copy-start.1
  5.4 14.9 %all-to-all-start = ((bf16[8,8,4096]{2,1,0:T(8,128)(2,1)}), bf16[8,8,4096]{2,1,0:T(8,128)(2,1)S(1)}, u32[]{:S(2)}, u32[]{:S(2)}) async-start(bf16[8,8,4096]{2,1,0:T(8,128)(2,1)} %fusion.9), calls=%async_computation | async-start | bytes 1048576 | tf_op jit(solution)/shard_map/all_to_all | solution.py:36
  32.7 19.1 %collective-permute-start.1 = (bf16[64,4096]{1,0:T(8,128)(2,1)S(1)}, bf16[64,4096]{1,0:T(8,128)(2,1)S(1)}, u32[]{:S(2)}, u32[]{:S(2)}) collective-permute-start(bf16[64,4096]{1,0:T(8,128)(2,1)S(1)} %fusion.53), channel_id=1, source_target_pairs={{120,0},{0,8},{8,16},{16,24},{24,32},{32,40},{40,48},{48,56},{56,6... | collective-permute-start | bytes 1572872 | tf_op jit(solution)/shard_map/while/body/eval_jaxpr/ppermute | solution.py:10
  34.7 27.3 %collective-permute-start = (bf16[64,4096]{1,0:T(8,128)(2,1)S(1)}, bf16[64,4096]{1,0:T(8,128)(2,1)S(1)}, u32[]{:S(2)}, u32[]{:S(2)}) collective-permute-start(bf16[64,4096]{1,0:T(8,128)(2,1)S(1)} %copy.60), channel_id=1, source_target_pairs={{120,0},{0,8},{8,16},{16,24},{24,32},{32,40},{40,48},{48,56},{56,6... | collective-permute-start | bytes 1572872 | tf_op jit(solution)/shard_map/while/body/eval_jaxpr/ppermute | solution.py:10
  74.4 18.2 %collective-permute-start.1 = (bf16[64,4096]{1,0:T(8,128)(2,1)S(1)}, bf16[64,4096]{1,0:T(8,128)(2,1)S(1)}, u32[]{:S(2)}, u32[]{:S(2)}) collective-permute-start(bf16[64,4096]{1,0:T(8,128)(2,1)S(1)} %fusion.53), channel_id=1, source_target_pairs={{120,0},{0,8},{8,16},{16,24},{24,32},{32,40},{40,48},{48,56},{56,6... | collective-permute-start | bytes 1572872 | tf_op jit(solution)/shard_map/while/body/eval_jaxpr/ppermute | solution.py:10
  74.4 27.4 %collective-permute-start = (bf16[64,4096]{1,0:T(8,128)(2,1)S(1)}, bf16[64,4096]{1,0:T(8,128)(2,1)S(1)}, u32[]{:S(2)}, u32[]{:S(2)}) collective-permute-start(bf16[64,4096]{1,0:T(8,128)(2,1)S(1)} %copy.60), channel_id=1, source_target_pairs={{120,0},{0,8},{8,16},{16,24},{24,32},{32,40},{40,48},{48,56},{56,6... | collective-permute-start | bytes 1572872 | tf_op jit(solution)/shard_map/while/body/eval_jaxpr/ppermute | solution.py:10
  114.3 18.3 %collective-permute-start.1 = (bf16[64,4096]{1,0:T(8,128)(2,1)S(1)}, bf16[64,4096]{1,0:T(8,128)(2,1)S(1)}, u32[]{:S(2)}, u32[]{:S(2)}) collective-permute-start(bf16[64,4096]{1,0:T(8,128)(2,1)S(1)} %fusion.53), channel_id=1, source_target_pairs={{120,0},{0,8},{8,16},{16,24},{24,32},{32,40},{40,48},{48,56},{56,6... | collective-permute-start | bytes 1572872 | tf_op jit(solution)/shard_map/while/body/eval_jaxpr/ppermute | solution.py:10
  114.4 26.5 %collective-permute-start = (bf16[64,4096]{1,0:T(8,128)(2,1)S(1)}, bf16[64,4096]{1,0:T(8,128)(2,1)S(1)}, u32[]{:S(2)}, u32[]{:S(2)}) collective-permute-start(bf16[64,4096]{1,0:T(8,128)(2,1)S(1)} %copy.60), channel_id=1, source_target_pairs={{120,0},{0,8},{8,16},{16,24},{24,32},{32,40},{40,48},{48,56},{56,6... | collective-permute-start | bytes 1572872 | tf_op jit(solution)/shard_map/while/body/eval_jaxpr/ppermute | solution.py:10
  153.3 18.3 %collective-permute-start.1 = (bf16[64,4096]{1,0:T(8,128)(2,1)S(1)}, bf16[64,4096]{1,0:T(8,128)(2,1)S(1)}, u32[]{:S(2)}, u32[]{:S(2)}) collective-permute-start(bf16[64,4096]{1,0:T(8,128)(2,1)S(1)} %fusion.53), channel_id=1, source_target_pairs={{120,0},{0,8},{8,16},{16,24},{24,32},{32,40},{40,48},{48,56},{56,6... | collective-permute-start | bytes 1572872 | tf_op jit(solution)/shard_map/while/body/eval_jaxpr/ppermute | solution.py:10
  153.4 25.6 %collective-permute-start = (bf16[64,4096]{1,0:T(8,128)(2,1)S(1)}, bf16[64,4096]{1,0:T(8,128)(2,1)S(1)}, u32[]{:S(2)}, u32[]{:S(2)}) collective-permute-start(bf16[64,4096]{1,0:T(8,128)(2,1)S(1)} %copy.60), channel_id=1, source_target_pairs={{120,0},{0,8},{8,16},{16,24},{24,32},{32,40},{40,48},{48,56},{56,6... | collective-permute-start | bytes 1572872 | tf_op jit(solution)/shard_map/while/body/eval_jaxpr/ppermute | solution.py:10
  191.3 18.2 %collective-permute-start.1 = (bf16[64,4096]{1,0:T(8,128)(2,1)S(1)}, bf16[64,4096]{1,0:T(8,128)(2,1)S(1)}, u32[]{:S(2)}, u32[]{:S(2)}) collective-permute-start(bf16[64,4096]{1,0:T(8,128)(2,1)S(1)} %fusion.53), channel_id=1, source_target_pairs={{120,0},{0,8},{8,16},{16,24},{24,32},{32,40},{40,48},{48,56},{56,6... | collective-permute-start | bytes 1572872 | tf_op jit(solution)/shard_map/while/body/eval_jaxpr/ppermute | solution.py:10
  191.4 24.7 %collective-permute-start = (bf16[64,4096]{1,0:T(8,128)(2,1)S(1)}, bf16[64,4096]{1,0:T(8,128)(2,1)S(1)}, u32[]{:S(2)}, u32[]{:S(2)}) collective-permute-start(bf16[64,4096]{1,0:T(8,128)(2,1)S(1)} %copy.60), channel_id=1, source_target_pairs={{120,0},{0,8},{8,16},{16,24},{24,32},{32,40},{40,48},{48,56},{56,6... | collective-permute-start | bytes 1572872 | tf_op jit(solution)/shard_map/while/body/eval_jaxpr/ppermute | solution.py:10
  228.5 18.2 %collective-permute-start.1 = (bf16[64,4096]{1,0:T(8,128)(2,1)S(1)}, bf16[64,4096]{1,0:T(8,128)(2,1)S(1)}, u32[]{:S(2)}, u32[]{:S(2)}) collective-permute-start(bf16[64,4096]{1,0:T(8,128)(2,1)S(1)} %fusion.53), channel_id=1, source_target_pairs={{120,0},{0,8},{8,16},{16,24},{24,32},{32,40},{40,48},{48,56},{56,6... | collective-permute-start | bytes 1572872 | tf_op jit(solution)/shard_map/while/body/eval_jaxpr/ppermute | solution.py:10
  228.6 23.7 %collective-permute-start = (bf16[64,4096]{1,0:T(8,128)(2,1)S(1)}, bf16[64,4096]{1,0:T(8,128)(2,1)S(1)}, u32[]{:S(2)}, u32[]{:S(2)}) collective-permute-start(bf16[64,4096]{1,0:T(8,128)(2,1)S(1)} %copy.60), channel_id=1, source_target_pairs={{120,0},{0,8},{8,16},{16,24},{24,32},{32,40},{40,48},{48,56},{56,6... | collective-permute-start | bytes 1572872 | tf_op jit(solution)/shard_map/while/body/eval_jaxpr/ppermute | solution.py:10
  264.7 17.3 %collective-permute-start.1 = (bf16[64,4096]{1,0:T(8,128)(2,1)S(1)}, bf16[64,4096]{1,0:T(8,128)(2,1)S(1)}, u32[]{:S(2)}, u32[]{:S(2)}) collective-permute-start(bf16[64,4096]{1,0:T(8,128)(2,1)S(1)} %fusion.53), channel_id=1, source_target_pairs={{120,0},{0,8},{8,16},{16,24},{24,32},{32,40},{40,48},{48,56},{56,6... | collective-permute-start | bytes 1572872 | tf_op jit(solution)/shard_map/while/body/eval_jaxpr/ppermute | solution.py:10
  264.8 22.8 %collective-permute-start = (bf16[64,4096]{1,0:T(8,128)(2,1)S(1)}, bf16[64,4096]{1,0:T(8,128)(2,1)S(1)}, u32[]{:S(2)}, u32[]{:S(2)}) collective-permute-start(bf16[64,4096]{1,0:T(8,128)(2,1)S(1)} %copy.60), channel_id=1, source_target_pairs={{120,0},{0,8},{8,16},{16,24},{24,32},{32,40},{40,48},{48,56},{56,6... | collective-permute-start | bytes 1572872 | tf_op jit(solution)/shard_map/while/body/eval_jaxpr/ppermute | solution.py:10
  300.0 16.4 %collective-permute-start.1 = (bf16[64,4096]{1,0:T(8,128)(2,1)S(1)}, bf16[64,4096]{1,0:T(8,128)(2,1)S(1)}, u32[]{:S(2)}, u32[]{:S(2)}) collective-permute-start(bf16[64,4096]{1,0:T(8,128)(2,1)S(1)} %fusion.53), channel_id=1, source_target_pairs={{120,0},{0,8},{8,16},{16,24},{24,32},{32,40},{40,48},{48,56},{56,6... | collective-permute-start | bytes 1572872 | tf_op jit(solution)/shard_map/while/body/eval_jaxpr/ppermute | solution.py:10
  300.1 21.9 %collective-permute-start = (bf16[64,4096]{1,0:T(8,128)(2,1)S(1)}, bf16[64,4096]{1,0:T(8,128)(2,1)S(1)}, u32[]{:S(2)}, u32[]{:S(2)}) collective-permute-start(bf16[64,4096]{1,0:T(8,128)(2,1)S(1)} %copy.60), channel_id=1, source_target_pairs={{120,0},{0,8},{8,16},{16,24},{24,32},{32,40},{40,48},{48,56},{56,6... | collective-permute-start | bytes 1572872 | tf_op jit(solution)/shard_map/while/body/eval_jaxpr/ppermute | solution.py:10
  334.4 15.4 %collective-permute-start.1 = (bf16[64,4096]{1,0:T(8,128)(2,1)S(1)}, bf16[64,4096]{1,0:T(8,128)(2,1)S(1)}, u32[]{:S(2)}, u32[]{:S(2)}) collective-permute-start(bf16[64,4096]{1,0:T(8,128)(2,1)S(1)} %fusion.53), channel_id=1, source_target_pairs={{120,0},{0,8},{8,16},{16,24},{24,32},{32,40},{40,48},{48,56},{56,6... | collective-permute-start | bytes 1572872 | tf_op jit(solution)/shard_map/while/body/eval_jaxpr/ppermute | solution.py:10
  334.5 21.0 %collective-permute-start = (bf16[64,4096]{1,0:T(8,128)(2,1)S(1)}, bf16[64,4096]{1,0:T(8,128)(2,1)S(1)}, u32[]{:S(2)}, u32[]{:S(2)}) collective-permute-start(bf16[64,4096]{1,0:T(8,128)(2,1)S(1)} %copy.60), channel_id=1, source_target_pairs={{120,0},{0,8},{8,16},{16,24},{24,32},{32,40},{40,48},{48,56},{56,6... | collective-permute-start | bytes 1572872 | tf_op jit(solution)/shard_map/while/body/eval_jaxpr/ppermute | solution.py:10
  367.8 14.5 %collective-permute-start.1 = (bf16[64,4096]{1,0:T(8,128)(2,1)S(1)}, bf16[64,4096]{1,0:T(8,128)(2,1)S(1)}, u32[]{:S(2)}, u32[]{:S(2)}) collective-permute-start(bf16[64,4096]{1,0:T(8,128)(2,1)S(1)} %fusion.53), channel_id=1, source_target_pairs={{120,0},{0,8},{8,16},{16,24},{24,32},{32,40},{40,48},{48,56},{56,6... | collective-permute-start | bytes 1572872 | tf_op jit(solution)/shard_map/while/body/eval_jaxpr/ppermute | solution.py:10
  367.9 20.0 %collective-permute-start = (bf16[64,4096]{1,0:T(8,128)(2,1)S(1)}, bf16[64,4096]{1,0:T(8,128)(2,1)S(1)}, u32[]{:S(2)}, u32[]{:S(2)}) collective-permute-start(bf16[64,4096]{1,0:T(8,128)(2,1)S(1)} %copy.60), channel_id=1, source_target_pairs={{120,0},{0,8},{8,16},{16,24},{24,32},{32,40},{40,48},{48,56},{56,6... | collective-permute-start | bytes 1572872 | tf_op jit(solution)/shard_map/while/body/eval_jaxpr/ppermute | solution.py:10
  400.4 13.6 %collective-permute-start.1 = (bf16[64,4096]{1,0:T(8,128)(2,1)S(1)}, bf16[64,4096]{1,0:T(8,128)(2,1)S(1)}, u32[]{:S(2)}, u32[]{:S(2)}) collective-permute-start(bf16[64,4096]{1,0:T(8,128)(2,1)S(1)} %fusion.53), channel_id=1, source_target_pairs={{120,0},{0,8},{8,16},{16,24},{24,32},{32,40},{40,48},{48,56},{56,6... | collective-permute-start | bytes 1572872 | tf_op jit(solution)/shard_map/while/body/eval_jaxpr/ppermute | solution.py:10
  400.5 19.1 %collective-permute-start = (bf16[64,4096]{1,0:T(8,128)(2,1)S(1)}, bf16[64,4096]{1,0:T(8,128)(2,1)S(1)}, u32[]{:S(2)}, u32[]{:S(2)}) collective-permute-start(bf16[64,4096]{1,0:T(8,128)(2,1)S(1)} %copy.60), channel_id=1, source_target_pairs={{120,0},{0,8},{8,16},{16,24},{24,32},{32,40},{40,48},{48,56},{56,6... | collective-permute-start | bytes 1572872 | tf_op jit(solution)/shard_map/while/body/eval_jaxpr/ppermute | solution.py:10
  432.0 12.7 %collective-permute-start.1 = (bf16[64,4096]{1,0:T(8,128)(2,1)S(1)}, bf16[64,4096]{1,0:T(8,128)(2,1)S(1)}, u32[]{:S(2)}, u32[]{:S(2)}) collective-permute-start(bf16[64,4096]{1,0:T(8,128)(2,1)S(1)} %fusion.53), channel_id=1, source_target_pairs={{120,0},{0,8},{8,16},{16,24},{24,32},{32,40},{40,48},{48,56},{56,6... | collective-permute-start | bytes 1572872 | tf_op jit(solution)/shard_map/while/body/eval_jaxpr/ppermute | solution.py:10
  432.1 18.2 %collective-permute-start = (bf16[64,4096]{1,0:T(8,128)(2,1)S(1)}, bf16[64,4096]{1,0:T(8,128)(2,1)S(1)}, u32[]{:S(2)}, u32[]{:S(2)}) collective-permute-start(bf16[64,4096]{1,0:T(8,128)(2,1)S(1)} %copy.60), channel_id=1, source_target_pairs={{120,0},{0,8},{8,16},{16,24},{24,32},{32,40},{40,48},{48,56},{56,6... | collective-permute-start | bytes 1572872 | tf_op jit(solution)/shard_map/while/body/eval_jaxpr/ppermute | solution.py:10
  462.7 12.6 %collective-permute-start.1 = (bf16[64,4096]{1,0:T(8,128)(2,1)S(1)}, bf16[64,4096]{1,0:T(8,128)(2,1)S(1)}, u32[]{:S(2)}, u32[]{:S(2)}) collective-permute-start(bf16[64,4096]{1,0:T(8,128)(2,1)S(1)} %fusion.53), channel_id=1, source_target_pairs={{120,0},{0,8},{8,16},{16,24},{24,32},{32,40},{40,48},{48,56},{56,6... | collective-permute-start | bytes 1572872 | tf_op jit(solution)/shard_map/while/body/eval_jaxpr/ppermute | solution.py:10
  462.8 18.1 %collective-permute-start = (bf16[64,4096]{1,0:T(8,128)(2,1)S(1)}, bf16[64,4096]{1,0:T(8,128)(2,1)S(1)}, u32[]{:S(2)}, u32[]{:S(2)}) collective-permute-start(bf16[64,4096]{1,0:T(8,128)(2,1)S(1)} %copy.60), channel_id=1, source_target_pairs={{120,0},{0,8},{8,16},{16,24},{24,32},{32,40},{40,48},{48,56},{56,6... | collective-permute-start | bytes 1572872 | tf_op jit(solution)/shard_map/while/body/eval_jaxpr/ppermute | solution.py:10
  493.3 12.6 %collective-permute-start.1 = (bf16[64,4096]{1,0:T(8,128)(2,1)S(1)}, bf16[64,4096]{1,0:T(8,128)(2,1)S(1)}, u32[]{:S(2)}, u32[]{:S(2)}) collective-permute-start(bf16[64,4096]{1,0:T(8,128)(2,1)S(1)} %fusion.53), channel_id=1, source_target_pairs={{120,0},{0,8},{8,16},{16,24},{24,32},{32,40},{40,48},{48,56},{56,6... | collective-permute-start | bytes 1572872 | tf_op jit(solution)/shard_map/while/body/eval_jaxpr/ppermute | solution.py:10
  493.3 18.1 %collective-permute-start = (bf16[64,4096]{1,0:T(8,128)(2,1)S(1)}, bf16[64,4096]{1,0:T(8,128)(2,1)S(1)}, u32[]{:S(2)}, u32[]{:S(2)}) collective-permute-start(bf16[64,4096]{1,0:T(8,128)(2,1)S(1)} %copy.60), channel_id=1, source_target_pairs={{120,0},{0,8},{8,16},{16,24},{24,32},{32,40},{40,48},{48,56},{56,6... | collective-permute-start | bytes 1572872 | tf_op jit(solution)/shard_map/while/body/eval_jaxpr/ppermute | solution.py:10
  523.9 12.6 %collective-permute-start.1 = (bf16[64,4096]{1,0:T(8,128)(2,1)S(1)}, bf16[64,4096]{1,0:T(8,128)(2,1)S(1)}, u32[]{:S(2)}, u32[]{:S(2)}) collective-permute-start(bf16[64,4096]{1,0:T(8,128)(2,1)S(1)} %fusion.53), channel_id=1, source_target_pairs={{120,0},{0,8},{8,16},{16,24},{24,32},{32,40},{40,48},{48,56},{56,6... | collective-permute-start | bytes 1572872 | tf_op jit(solution)/shard_map/while/body/eval_jaxpr/ppermute | solution.py:10
  523.9 18.1 %collective-permute-start = (bf16[64,4096]{1,0:T(8,128)(2,1)S(1)}, bf16[64,4096]{1,0:T(8,128)(2,1)S(1)}, u32[]{:S(2)}, u32[]{:S(2)}) collective-permute-start(bf16[64,4096]{1,0:T(8,128)(2,1)S(1)} %copy.60), channel_id=1, source_target_pairs={{120,0},{0,8},{8,16},{16,24},{24,32},{32,40},{40,48},{48,56},{56,6... | collective-permute-start | bytes 1572872 | tf_op jit(solution)/shard_map/while/body/eval_jaxpr/ppermute | solution.py:10
  554.4 12.6 %collective-permute-start.2 = (bf16[64,4096]{1,0:T(8,128)(2,1)S(1)}, bf16[64,4096]{1,0:T(8,128)(2,1)S(1)}, u32[]{:S(2)}, u32[]{:S(2)}) collective-permute-start(bf16[64,4096]{1,0:T(8,128)(2,1)S(1)} %add_convert_fusion), channel_id=1, source_target_pairs={{120,0},{0,8},{8,16},{16,24},{24,32},{32,40},{40,48},{48,56},{56,6... | collective-permute-start | bytes 1572872 | tf_op jit(solution)/shard_map/ppermute | solution.py:10
where the time goes:
time: 585 us; the launch traced here: 583 us
  waiting for transfers between devices  351 us (60%)
  matrix products  198 us (34%)
  blocking collectives  15.5 us (3%)
  starting transfers between devices  10.6 us (2%)
    ppermute x31, waiting for transfers between devices, from_behind(): return lax.ppermute(block, axis, route)  341 us
    dot_general x16, matrix products, section_term(): jnp.dot(hidden, w_down, preferred_element_type=jnp.float32)  126 us
    dot_general x16, matrix products, section_term(): gate_act = jnp.dot(block_rows, w_gate, preferred_element_type=jnp.float32)  69.1 us
    all_to_all x1, blocking collectives, shards(): lax.all_to_all(expert_out, 'expert', split_axis=0, concat_axis=0, tiled=T...  15.5 us
  transfers between devices with their start and end apart: 32, of which 32 were waited for; matrix products, arithmetic and copies ran while one was open for 0% of the time, Pallas kernels for 0%

commit v1 on v0

--- a/solution.py
+++ b/solution.py
@@ -2,12 +2,6 @@
 import jax.numpy as jnp
 from jax import lax
 from jax.sharding import PartitionSpec as P
-
-
-def from_behind(block, axis, distance):
-    devices = range(lax.axis_size(axis))
-    route = [((i - distance) % len(devices), i) for i in devices]
-    return lax.ppermute(block, axis, route)
 
 
 def shards(tokens, routes, router_weight, gate_weight, up_weight, down_weight):
@@ -35,35 +29,13 @@
     outgoing = outgoing.reshape(experts, capacity, width_model)
     received = lax.all_to_all(outgoing, "expert", split_axis=0, concat_axis=0, tiled=True)
     arrived = received.reshape(-1, width_model)
-    w_gate = gate_weight[0]
-    w_up = up_weight[0]
-    w_down = down_weight[0]
-
-    def section_term(block_rows):
-        gate_act = jnp.dot(block_rows, w_gate, preferred_element_type=jnp.float32)
-        up_act = jnp.dot(block_rows, w_up, preferred_element_type=jnp.float32)
-        hidden = (jax.nn.silu(gate_act) * up_act).astype(jnp.bfloat16)
-        partial_sum = jnp.dot(hidden, w_down, preferred_element_type=jnp.float32).astype(
-            jnp.bfloat16
-        )
-        partial_sum = lax.optimization_barrier(partial_sum)
-        return partial_sum.astype(jnp.float32)
-
-    sections = lax.axis_size("section")
-
-    def pass_sums(running):
-        return from_behind(running.astype(jnp.bfloat16), "section", 1).astype(running.dtype)
-
-    def one_step(position, state_pair):
-        rows_now, running = state_pair
-        running = pass_sums(running + section_term(rows_now))
-        rows_now = from_behind(rows_now, "section", 1)
-        return (rows_now, running)
-
-    start_sum = jnp.zeros(arrived.shape, jnp.float32)
-    rows_now, running = lax.fori_loop(0, sections - 1, one_step, (arrived, start_sum))
-    summed = pass_sums(running + section_term(rows_now))
-    expert_out = summed.astype(jnp.bfloat16).reshape(experts, capacity, width_model)
+    rows = lax.all_gather(arrived, "section", axis=0, tiled=True)
+    gate_act = jnp.dot(rows, gate_weight[0], preferred_element_type=jnp.float32)
+    up_act = jnp.dot(rows, up_weight[0], preferred_element_type=jnp.float32)
+    hidden = (jax.nn.silu(gate_act) * up_act).astype(jnp.bfloat16)
+    partial_sum = jnp.dot(hidden, down_weight[0], preferred_element_type=jnp.float32).astype(jnp.bfloat16)
+    summed = lax.psum_scatter(partial_sum, "section", scatter_dimension=0, tiled=True)
+    expert_out = summed.reshape(experts, capacity, width_model)
     returned = lax.all_to_all(expert_out, "expert", split_axis=0, concat_axis=0, tiled=True)
     combine = jnp.sum(gate_pair[:, :, None] * placing, axis=1)
     mixed = jnp.dot(

time: 585 us -> 241 us (0.41)
  waiting for transfers between devices: 351 us -> 156 us
  matrix products: 198 us -> 37.9 us
  blocking collectives: 15.5 us -> 29.6 us
  between operations: 0.08 us -> 13.5 us
  starting transfers between devices: 10.6 us -> 0.04 us
    ppermute x31 -> x0, waiting for transfers between devices: 341 us -> none  [from_behind(): return lax.ppermute(block, axis, route)]
    dot_general x32 -> x3, matrix products: 195 us -> 35.6 us  [the longest x1 12.5 us: shards(): up_act = jnp.dot(rows, up_weight[0], preferred_element_type=jnp.float32)]
    reduce_scatter x0 -> x1, waiting for transfers between devices: none -> 84.9 us  [shards(): lax.psum_scatter(partial_sum, 'section', scatter_dimension=0, tiled=True)]
    all_gather x0 -> x1, waiting for transfers between devices: none -> 71.3 us  [shards(): rows = lax.all_gather(arrived, 'section', axis=0, tiled=True)]
    all_to_all x0 -> x1, blocking collectives: none -> 14.8 us  [shards(): lax.all_to_all(outgoing, 'expert', split_axis=0, concat_axis=0, tiled=True)]
    all_to_all x1 -> x0, waiting for transfers between devices: 10.3 us -> none  [shards(): lax.all_to_all(outgoing, 'expert', split_axis=0, concat_axis=0, tiled=True)]
    ppermute x31 -> x0, starting transfers between devices: 6.09 us -> none  [from_behind(): return lax.ppermute(block, axis, route)]
  transfers between devices with their start and end apart: 32 -> 2, of which waited for: 32 -> 2; matrix products, arithmetic and copies ran while one was open for 0% -> 0% of each run, Pallas kernels for 0% -> 0%
where the time goes in v1:
time: 241 us
  waiting for transfers between devices  156 us (65%)
  matrix products  37.9 us (16%)
  blocking collectives  29.6 us (12%)
  between operations  13.5 us (6%)
    reduce_scatter x1, waiting for transfers between devices, shards(): lax.psum_scatter(partial_sum, 'section', scatter_dimension=0, tiled=True)  84.9 us
    all_gather x1, waiting for transfers between devices, shards(): rows = lax.all_gather(arrived, 'section', axis=0, tiled=True)  71.3 us
    all_to_all x1, blocking collectives, shards(): lax.all_to_all(outgoing, 'expert', split_axis=0, concat_axis=0, tiled=True)  14.8 us
    all_to_all x1, blocking collectives, shards(): lax.all_to_all(expert_out, 'expert', split_axis=0, concat_axis=0, tiled=T...  14.7 us
    dot_general x1, matrix products, shards(): up_act = jnp.dot(rows, up_weight[0], preferred_element_type=jnp.float32)  12.5 us
    dot_general x1, matrix products, shards(): gate_act = jnp.dot(rows, gate_weight[0], preferred_element_type=jnp.float32)  12.1 us
    dot_general x1, matrix products, shards(): jnp.dot(hidden, down_weight[0], preferred_element_type=jnp.float32)  11.1 us
  transfers between devices with their start and end apart: 2, of which 2 were waited for; matrix products, arithmetic and copies ran while one was open for 0% of the time, Pallas kernels for 0%

profile of v1, /device:TPU:0, one launch (start us, length us, event | category | flops | bytes accessed | tf_op | source)
XLA Modules:
  0.0 240.5 jit_solution(5048860163323709414)
XLA Ops:
  6.5 0.0 copy-start
  6.5 0.0 copy-start.1
  6.5 0.0 all-gather.2.cloned.1.call-start
  6.5 0.8 bitcast_or_fusion
  7.3 0.8 copy.52
  8.1 0.1 copy.54
  8.1 0.1 reshape.36
  8.2 0.0 copy-done
  8.2 1.0 fusion.11
  9.2 0.7 gather_fusion
  9.9 0.1 reshape.39
  10.0 0.1 copy.55
  10.1 0.0 copy-done.1
  10.1 0.1 eq.29
  10.2 0.1 fusion.9
  10.3 0.1 reduce_window_sum.11
  10.3 0.2 select_reduce_fusion.1
  10.5 0.1 reshape.30
  10.6 0.1 copy.53
  10.7 0.1 convert_reduce_fusion
  10.8 0.3 fusion.5
  11.1 14.8 %all_to_all.10 = bf16[8,8,4096]{2,1,0:T(8,128)(2,1)} all-to-all(bf16[8,8,4096]{2,1,0:T(8,128)(2,1)S(1)} %fusion.5), channel_id=1, replica_groups=mesh['section'=16,'expert'=8] {'expert'}, dimensions={0} | all-to-all | bytes 1048576 | tf_op jit(solution)/shard_map/all_to_all | solution.py:30
  26.0 0.0 all-gather.2.cloned.1.call-update
  26.0 0.0 reduce-scatter.2.cloned.1.call-start
  26.1 71.3 %all-gather.2.cloned.1.call-done = bf16[1024,4096]{1,0:T(8,128)(2,1)} async-done(((bf16[64,4096]{1,0:T(8,128)(2,1)}), bf16[1024,4096]{1,0:T(8,128)(2,1)}) %all-gather.2.cloned.1.call-update) | async-done | bytes 8388624 | tf_op jit(solution)/shard_map/all_gather | solution.py:32
  97.4 0.0 copy-start.2
  97.4 0.0 slice-start
  97.4 12.5 %fusion.1 = f32[1024,896]{1,0:T(8,128)S(1)} fusion(bf16[1024,4096]{1,0:T(8,128)(2,1)} %all-gather.2.cloned.1.call-done, bf16[1,4096,896]{2,1,0:T(8,128)(2,1)} %param.10), kind=kOutput, calls=%fused_computation.3 | convolution fusion | flops 7516192768 | bytes 19398656 | tf_op jit(solution)/shard_map/dot_general | solution.py:34
  109.9 0.0 copy-done.2
  109.9 0.0 slice-start.1
  109.9 12.1 %multiply_convert_fusion = bf16[1024,896]{1,0:T(8,128)(2,1)S(1)} fusion(f32[1024,896]{1,0:T(8,128)S(1)} %fusion.1, bf16[1024,4096]{1,0:T(8,128)(2,1)S(1)} %copy-done.2, bf16[1,4096,896]{2,1,0:T(8,128)(2,1)} %param.9), kind=kOutput, calls=%fused_computation.10 | convolution fusion | flops 7521697792 | bytes 21233664 | tf_op jit(solution)/shard_map/dot_general | solution.py:33
  122.0 0.0 slice-done
  122.0 0.0 slice-done.1
  122.0 11.1 %convolution_convert_fusion = bf16[1024,4096]{1,0:T(8,128)(2,1)} fusion(bf16[1024,896]{1,0:T(8,128)(2,1)S(1)} %multiply_convert_fusion, bf16[1,896,4096]{2,1,0:T(8,128)(2,1)S(1)} %bitcast.33), kind=kOutput, calls=%fused_computation.1 | convolution fusion | flops 7520387072 | bytes 17563648 | tf_op jit(solution)/shard_map/dot_general | solution.py:36
  133.1 0.0 reduce-scatter.2.cloned.1.call-update
  133.1 84.9 %reduce-scatter.2.cloned.1.call-done = bf16[64,4096]{1,0:T(8,128)(2,1)} async-done(((bf16[1024,4096]{1,0:T(8,128)(2,1)}), bf16[64,4096]{1,0:T(8,128)(2,1)}) %reduce-scatter.2.cloned.1.call-update) | async-done | bytes 524304 | tf_op jit(solution)/shard_map/reduce_scatter | solution.py:37
  218.0 14.7 %all_to_all.11 = bf16[8,8,4096]{2,1,0:T(8,128)(2,1)S(1)} all-to-all(bf16[8,8,4096]{2,1,0:T(8,128)(2,1)} %bitcast.31), channel_id=1, replica_groups=mesh['section'=16,'expert'=8] {'expert'}, dimensions={0} | all-to-all | bytes 1048576 | tf_op jit(solution)/shard_map/all_to_all | solution.py:39
  232.7 1.0 convolution_convert_fusion.2
  (5 shorter events, 0.0 us)
Async XLA Ops:
  6.5 1.7 copy-start
  6.5 3.5 %copy-start.1 = (s32[16,2]{0,1:T(2,128)S(1)}, s32[16,2]{0,1:T(2,128)}, u32[]{:S(2)}) copy-start(s32[16,2]{0,1:T(2,128)} %param.7) | copy-start | bytes 388
  6.5 90.8 %all-gather.2.cloned.1.call-start = ((), (), s32[]{:S(2)}) async-start(), calls=%async_computation.3 | async-start | bytes 8912896 | tf_op jit(solution)/shard_map/all_gather | solution.py:32
  26.0 192.0 %reduce-scatter.2.cloned.1.call-start = ((), (), s32[]{:S(2)}) async-start(), calls=%async_computation.4 | async-start | bytes 8912896 | tf_op jit(solution)/shard_map/reduce_scatter | solution.py:37
  97.4 12.5 %copy-start.2 = (bf16[1024,4096]{1,0:T(8,128)(2,1)S(1)}, bf16[1024,4096]{1,0:T(8,128)(2,1)}, u32[]{:S(2)}) copy-start(bf16[1024,4096]{1,0:T(8,128)(2,1)} %all-gather.2.cloned.1.call-done) | copy-start | bytes 25165828
  97.4 24.6 %slice-start = ((s8[7340032]{0:T(1024)(128)(4,1)}), s8[4194304]{0:T(1024)(128)(4,1)S(1)}, s32[]{:S(2)}) async-start(s8[7340032]{0:T(1024)(128)(4,1)} %bitcast.32), calls=%async_computation.5 | async-start | bytes 8388608
  109.9 12.1 %slice-start.1 = ((s8[7340032]{0:T(1024)(128)(4,1)}), s8[3145728]{0:T(1024)(128)(4,1)S(1)}, s32[]{:S(2)}) async-start(s8[7340032]{0:T(1024)(128)(4,1)} %bitcast.32), calls=%async_computation.6 | async-start | bytes 6291456
Sparse Core Ops, SparseCore 0:
  26.1 71.2 all-gather.1
  133.2 84.7 reduce-scatter.1

commit v2 on v1

v2 whole, which is shorter than its diff:
```python
import jax
import jax.numpy as jnp
from jax import lax
from jax.experimental import pallas as pl
from jax.experimental.pallas import tpu as pltpu
from jax.sharding import PartitionSpec as P

MESH = pl.DeviceIdType.MESH
F32, BF16 = jnp.float32, jnp.bfloat16
SIDE = 4
COLOURS = ((0, 1408), (1408, 1408), (2816, 1280))
LANES = 128
VMEM_BYTES = 64 * 1024 * 1024 - 65536


def column_half(start, size, half):
    first = (size // LANES + 1) // 2 * LANES
    return (start, first) if half == 0 else (start + first, size - first)


def spread_dims(colour, phase):
    return sorted((colour + j) % 3 for j in range(phase))


def kernel(x_ref, routes_ref, router_ref, wg_ref, wu_ref, wd_ref, out_ref,
           wgu, wd, rows, meta, xs, staging, acts, hidden, back,
           ra2, rb2, ra1, rb1, ra0, rb0,
           w_sem, ag_send, ag_recv, meta_send, meta_recv, in_send, in_recv, back_send, back_recv,
           rs_send, rs_recv):
    section, expert = lax.axis_index("section"), lax.axis_index("expert")
    core = lax.rem(expert, 2)
    pos = [lax.div(section, SIDE), lax.div(expert, 2), lax.rem(section, SIDE)]
    width = x_ref.shape[1]
    ff = wg_ref.shape[1]
    other_expert = pos[1] * 2 + 1 - core
    twin = (section, other_expert)

    def step(dim, off):
        return lax.rem(pos[dim] + off + SIDE, SIDE)

    def near(dim, off):
        p = list(pos)
        p[dim] = step(dim, off)
        return (p[0] * SIDE + p[2], p[1] * 2 + core)

    loads = [
        pltpu.make_async_copy(wg_ref, wgu.at[:, pl.ds(0, ff)], w_sem.at[0]),
        pltpu.make_async_copy(wu_ref, wgu.at[:, pl.ds(ff, ff)], w_sem.at[1]),
        pltpu.make_async_copy(wd_ref, wd, w_sem.at[2]),
    ]
    for load in loads:
        load.start()

    barrier = pltpu.get_barrier_semaphore()
    greeted = [near(d, o) for d in range(3) for o in (1, -1)] + [twin]
    for device in greeted:
        pl.semaphore_signal(barrier, inc=1, device_id=device, device_id_type=MESH)

    rows[pos[0], pos[1], pos[2]] = x_ref[...]

    tok = x_ref.shape[0]
    logits = lax.dot_general(x_ref[...], router_ref[...], (((1,), (1,)), ((), ())),
                             preferred_element_type=F32)
    first, second = routes_ref[:, 0:1], routes_ref[:, 1:2]
    narrow = lax.broadcasted_iota(jnp.int32, logits.shape, 1)
    gap = (jnp.sum(jnp.where(narrow == first, logits, 0.0), axis=1, keepdims=True)
           - jnp.sum(jnp.where(narrow == second, logits, 0.0), axis=1, keepdims=True))
    gate0 = jax.nn.sigmoid(gap)
    gate1 = 1.0 - gate0
    lane = lax.broadcasted_iota(jnp.int32, (tok, LANES), 1)
    named = jnp.where(lane == first, 1.0, 0.0) + jnp.where(lane == second, 1.0, 0.0)
    below = jnp.where(lax.broadcasted_iota(jnp.int32, (tok, tok), 0)
                      > lax.broadcasted_iota(jnp.int32, (tok, tok), 1), 1.0, 0.0)
    earlier = jnp.dot(below.astype(BF16), named.astype(BF16), preferred_element_type=F32)
    facts = (named * (earlier + 1.0) + jnp.where(lane == first + 8, gate0, 0.0)
             + jnp.where(lane == second + 8, gate1, 0.0))
    meta[pos[0], pos[1], pos[2]] = facts.astype(BF16)

    pl.semaphore_wait(barrier, len(greeted))

    def send(src, dst, sends, recvs, n, device):
        copy = pltpu.make_async_remote_copy(src_ref=src, dst_ref=dst, send_sem=sends.at[n], recv_sem=recvs.at[n],
                                            device_id=device, device_id_type=MESH)
        copy.start()
        return copy

    def piece(ref, colour, phase, at, half):
        start, size = COLOURS[colour]
        dims = spread_dims(colour, phase)
        index = list(pos)
        index[(colour + phase) % 3] = at
        for n, d in enumerate(dims):
            index[d] = pl.ds(0, SIDE)
            if n == 0 and half is not None:
                index[d] = pl.ds(2 * half, 2)
        if phase == 0 and half is not None:
            start, size = column_half(start, size, half)
        return ref.at[index[0], index[1], index[2], :, pl.ds(start, size)]

    pending = []
    for phase in range(3):
        meta_dim = phase
        mi = list(pos)
        for d in range(phase):
            mi[d] = pl.ds(0, SIDE)

        def meta_piece(at):
            index = list(mi)
            index[meta_dim] = at
            return meta.at[index[0], index[1], index[2]]

        mine = meta_piece(pos[meta_dim])
        m_right = send(mine, mine, meta_send, meta_recv, 3 * phase, near(meta_dim, 1))
        m_left = send(mine, mine, meta_send, meta_recv, 3 * phase + 1, near(meta_dim, -1))
        firsts = []
        for colour in range(3):
            dim = (colour + phase) % 3
            base = (phase * 3 + colour) * 6
            got = {}
            for n, (off, half) in enumerate(((1, 0), (-1, 1), (1, 1), (-1, 0))):
                view = piece(rows, colour, phase, pos[dim], half)
                got[off, half] = send(view, view, ag_send, ag_recv, base + n, near(dim, off))
            firsts.append(got)
        m_right.wait_recv()
        view = meta_piece(step(meta_dim, -1))
        m_far = send(view, view, meta_send, meta_recv, 3 * phase + 2, near(meta_dim, 1))
        relays = []
        for colour in range(3):
            dim = (colour + phase) % 3
            base = (phase * 3 + colour) * 6
            for n, (off, half) in enumerate(((1, 0), (-1, 1))):
                firsts[colour][off, half].wait_recv()
                view = piece(rows, colour, phase, step(dim, -off), half)
                relays.append(send(view, view, ag_send, ag_recv, base + 4 + n, near(dim, off)))
        m_left.wait_recv()
        m_far.wait_recv()
        for colour in range(3):
            firsts[colour][1, 1].wait_recv()
            firsts[colour][-1, 0].wait_recv()
        for copy in relays:
            copy.wait_recv()
        pending += [m_right, m_left, m_far] + relays + [c for got in firsts for c in got.values()]
    for copy in pending:
        copy.wait_send()

    groups = 8
    span = 64
    wide = lax.broadcasted_iota(jnp.int32, (LANES, LANES), 1)
    tall = lax.broadcasted_iota(jnp.int32, (LANES, LANES), 0)
    block_of = (lax.div(tall, tok) * 8).astype(F32)[:, 0:1]
    wide_f = wide.astype(F32)

    def placing(g, weighted):
        facts = meta[lax.div(g, 2), pl.ds(lax.rem(g, 2) * 2, 2)].reshape(LANES, LANES).astype(F32)
        total = jnp.zeros((LANES, LANES), F32)
        for which, base in ((expert, 0.0), (other_expert, float(span))):
            slot = jnp.sum(jnp.where(wide == which, facts, 0.0), axis=1, keepdims=True)
            place = jnp.where(slot > 0.5, block_of + slot + (base - 1.0), -1.0)
            value = 1.0
            if weighted:
                value = jnp.sum(jnp.where(wide == which + 8, facts, 0.0), axis=1, keepdims=True)
            total = total + jnp.where(wide_f == place, value, 0.0)
        return total.astype(BF16)

    chunk = 1024
    half_rows = groups * span

    def pick(g, carry):
        place = placing(g, False)
        for n in range(width // chunk):
            cols = pl.ds(n * chunk, chunk)
            block = rows[lax.div(g, 2), pl.ds(lax.rem(g, 2) * 2, 2), :, :, cols].reshape(LANES, chunk)
            got = lax.dot_general(place, block, (((0,), (0,)), ((), ())),
                                  preferred_element_type=F32).astype(BF16)
            xs[pl.ds(pl.multiple_of(g * span, span), span), cols] = got[:span]
            staging[pl.ds(pl.multiple_of(g * span, span), span), cols] = got[span:]
        return carry

    lax.fori_loop(0, groups, pick, 0)
    over = [send(staging.at[pl.ds(q * 256, 256)], xs.at[pl.ds(half_rows + q * 256, 256)],
                 in_send, in_recv, q, twin) for q in range(2)]

    loads[0].wait()
    loads[1].wait()
    tile = 512
    n_tile = 256

    def up_projection(r):
        def one(n, carry):
            cols = pl.ds(pl.multiple_of(n * n_tile, n_tile), n_tile)
            acts[:, cols] = jnp.dot(xs[pl.ds(r * tile, tile)], wgu[:, cols], preferred_element_type=F32)
            return carry

        lax.fori_loop(0, 2 * ff // n_tile, one, 0)

        def squash(i, carry):
            at = pl.ds(pl.multiple_of(i * 32, 32), 32)
            gate = acts[at, pl.ds(0, ff)]
            value = gate / (1.0 + jnp.exp(-gate)) * acts[at, pl.ds(ff, ff)]
            hidden[pl.ds(pl.multiple_of(r * tile + i * 32, 32), 32)] = value.astype(BF16)
            return carry

        lax.fori_loop(0, tile // 32, squash, 0)

    up_projection(0)
    for copy in over:
        copy.wait()
    up_projection(1)
    loads[2].wait()

    returns = []
    quarter = width // 4
    for q in range(4):
        def theirs(n, carry, q=q):
            cols = pl.ds(pl.multiple_of(q * quarter + n * n_tile, n_tile), n_tile)
            staging[:, cols] = jnp.dot(hidden[pl.ds(half_rows, half_rows)], wd[:, cols],
                                       preferred_element_type=F32).astype(BF16)
            return carry

        lax.fori_loop(0, quarter // n_tile, theirs, 0)
        cols = pl.ds(q * quarter, quarter)
        returns.append(send(staging.at[:, cols], back.at[:, cols], back_send, back_recv, q, twin))

    def mine(n, carry):
        cols = pl.ds(pl.multiple_of(n * n_tile, n_tile), n_tile)
        xs[pl.ds(0, half_rows), cols] = jnp.dot(hidden[pl.ds(0, half_rows)], wd[:, cols],
                                                preferred_element_type=F32).astype(BF16)
        return carry

    lax.fori_loop(0, width // n_tile, mine, 0)
    for copy in returns:
        copy.wait()

    def mix(g, carry):
        place = placing(g, True)
        at = pl.ds(pl.multiple_of(g * span, span), span)
        for n in range(width // chunk):
            cols = pl.ds(n * chunk, chunk)
            both = jnp.concatenate([xs[at, cols], back[at, cols]], axis=0)
            got = jnp.dot(place, both, preferred_element_type=F32).astype(BF16)
            rows[lax.div(g, 2), pl.ds(lax.rem(g, 2) * 2, 2), :, :, cols] = got.reshape(2, SIDE, tok, chunk)
        return carry

    lax.fori_loop(0, groups, mix, 0)

    def landing(ref, colour, phase, way, half):
        start, size = COLOURS[colour]
        if phase == 0:
            if half is not None:
                start, size = column_half(start, size, half)
            return ref.at[way, :, pl.ds(start, size)]
        lead = pl.ds(0, ref.shape[1]) if half is None else pl.ds(2 * half, 2)
        if phase == 1:
            return ref.at[way, lead, :, pl.ds(start, size)]
        return ref.at[way, lead, :, :, pl.ds(start, size)]

    def add_in(colour, phase, at, half, parts):
        start, size = COLOURS[colour]
        dims = spread_dims(colour, phase)
        if phase == 0 and half is not None:
            start, size = column_half(start, size, half)
        cols = pl.ds(start, size)

        def one(i, carry):
            index = list(pos)
            index[(colour + phase) % 3] = at
            if phase == 2:
                lead, low = lax.div(i, SIDE), lax.rem(i, SIDE)
                index[dims[1]] = low
            else:
                lead, low = i, None
            if phase >= 1:
                index[dims[0]] = lead if half is None else lead + 2 * half
            total = rows[index[0], index[1], index[2], :, cols].astype(F32)
            for ref, way in parts:
                if phase == 0:
                    total = total + ref[way, :, cols].astype(F32)
                elif phase == 1:
                    total = total + ref[way, lead, :, cols].astype(F32)
                else:
                    total = total + ref[way, lead, low, :, cols].astype(F32)
            rows[index[0], index[1], index[2], :, cols] = total.astype(BF16)
            return carry

        count = (SIDE if half is None else 2) if phase >= 1 else 1
        count = count * SIDE if phase == 2 else count
        lax.fori_loop(0, count, one, 0)

    pending = []
    for phase, ra, rb in ((2, ra2, rb2), (1, ra1, rb1), (0, ra0, rb0)):
        fars, seconds = [], []
        for colour in range(3):
            dim = (colour + phase) % 3
            base = (phase * 3 + colour) * 6
            far, second = {}, {}
            for n, (off, half, way) in enumerate(((1, 0, 0), (-1, 1, 1))):
                far[off] = send(piece(rows, colour, phase, step(dim, 2), half),
                                landing(ra, colour, phase, way, half if phase == 0 else None),
                                rs_send, rs_recv, base + n, near(dim, off))
            for n, (off, half, way) in enumerate(((1, 1, 0), (-1, 0, 1))):
                second[off, half] = send(piece(rows, colour, phase, step(dim, off), half),
                                         landing(rb, colour, phase, way, half),
                                         rs_send, rs_recv, base + 2 + n, near(dim, off))
            fars.append(far)
            seconds.append(second)
        for colour in range(3):
            dim = (colour + phase) % 3
            base = (phase * 3 + colour) * 6
            for n, (off, half, way) in enumerate(((1, 0, 0), (-1, 1, 1))):
                fars[colour][off].wait_recv()
                add_in(colour, phase, step(dim, off), half, [(ra, way)])
                seconds[colour][off, half] = send(piece(rows, colour, phase, step(dim, off), half),
                                                  landing(rb, colour, phase, way, half),
                                                  rs_send, rs_recv, base + 4 + n, near(dim, off))
        for colour in range(3):
            dim = (colour + phase) % 3
            for copy in seconds[colour].values():
                copy.wait_recv()
            add_in(colour, phase, pos[dim], None, [(rb, 0), (rb, 1)])
        pending += [c for far in fars for c in far.values()] + [c for sec in seconds for c in sec.values()]
    for copy in pending:
        copy.wait_send()
    out_ref[...] = rows[pos[0], pos[1], pos[2]]


def shards(tokens, routes, router_weight, gate_weight, up_weight, down_weight):
    tok, width = tokens.shape
    ff = gate_weight.shape[2]
    blocks = (SIDE, SIDE, SIDE)
    vmem = pl.BlockSpec(memory_space=pltpu.VMEM)
    anywhere = pl.BlockSpec(memory_space=pl.ANY)
    dma = pltpu.SemaphoreType.DMA
    return pl.pallas_call(
        kernel,
        out_shape=jax.ShapeDtypeStruct((tok, width), BF16),
        in_specs=[vmem, vmem, vmem, anywhere, anywhere, anywhere],
        out_specs=vmem,
        scratch_shapes=[
            pltpu.VMEM((width, 2 * ff), BF16),
            pltpu.VMEM((ff, width), BF16),
            pltpu.VMEM(blocks + (tok, width), BF16),
            pltpu.VMEM(blocks + (tok, LANES), BF16),
            pltpu.VMEM((1024, width), BF16),
            pltpu.VMEM((512, width), BF16),
            pltpu.VMEM((512, 2 * ff), F32),
            pltpu.VMEM((1024, ff), BF16),
            pltpu.VMEM((512, width), BF16),
            pltpu.VMEM((2, 2, SIDE, tok, width), BF16),
            pltpu.VMEM((2, SIDE, SIDE, tok, width), BF16),
            pltpu.VMEM((2, 2, tok, width), BF16),
            pltpu.VMEM((2, SIDE, tok, width), BF16),
            pltpu.VMEM((2, tok, width), BF16),
            pltpu.VMEM((2, tok, width), BF16),
            dma((3,)),
            dma((54,)), dma((54,)),
            dma((9,)), dma((9,)),
            dma((2,)), dma((2,)),
            dma((4,)), dma((4,)),
            dma((54,)), dma((54,)),
        ],
        compiler_params=pltpu.CompilerParams(
            collective_id=0, has_side_effects=True, vmem_limit_bytes=VMEM_BYTES
        ),
        cost_estimate=pl.CostEstimate(flops=2 * 3 * 1024 * width * ff, bytes_accessed=6 * ff * width,
                                      transcendentals=1024 * ff),
    )(tokens, routes, router_weight.T, gate_weight[0], up_weight[0], down_weight[0])


def solution(mesh):
    in_specs = (
        P(("section", "expert"), None),
        P(("section", "expert"), None),
        P(),
        P("expert", None, "section"),
        P("expert", None, "section"),
        P("expert", "section", None),
    )
    out_specs = P(("section", "expert"), None)
    return jax.shard_map(shards, mesh=mesh, in_specs=in_specs, out_specs=out_specs, check_vma=False)
```

time: 241 us -> 138 us (0.57)
  waiting for transfers between devices: 156 us -> 0 us
  Pallas kernels: 0 us -> 135 us
  matrix products: 37.9 us -> 0 us
  blocking collectives: 29.6 us -> 0 us
  between operations: 13.5 us -> 0.01 us
    pallas_call x0 -> x1, Pallas kernels: none -> 135 us  [shards(): pl.pallas_call(kernel, out_shape=jax.ShapeDtypeStruct((tok, width), BF16)...]
    reduce_scatter x1 -> x0, waiting for transfers between devices: 84.9 us -> none  [shards(): lax.psum_scatter(partial_sum, 'section', scatter_dimension=0, tiled=True)]
    all_gather x1 -> x0, waiting for transfers between devices: 71.3 us -> none  [shards(): rows = lax.all_gather(arrived, 'section', axis=0, tiled=True)]
    dot_general x6 -> x0, matrix products: 37.9 us -> none  [the longest x1 12.5 us: shards(): up_act = jnp.dot(rows, up_weight[0], preferred_element_type=jnp.float32)]
    all_to_all x2 -> x0, blocking collectives: 29.6 us -> none  [the longest x1 14.8 us: shards(): lax.all_to_all(outgoing, 'expert', split_axis=0, concat_axis=0, tiled=True)]
  transfers between devices with their start and end apart: 2 -> 0, of which waited for: 2 -> 0; matrix products, arithmetic and copies ran while one was open for 0% -> 0% of each run, Pallas kernels for 0% -> 0%
where the time goes in v2:
time: 138 us
  Pallas kernels  135 us (98%)
  local copies, waits for them, and re-layouts  2.92 us (2%)
    pallas_call x1, Pallas kernels, shards(): pl.pallas_call(kernel, out_shape=jax.ShapeDtypeStruct((tok, width), BF16)...  135 us
    unnamed x2, local copies, waits for them, and re-layouts  2.92 us

profile of v2, /device:TPU:0, one launch (start us, length us, event | category | flops | bytes accessed | tf_op | source)
XLA Modules:
  0.0 137.9 jit_solution(8866631004405264814)
XLA Ops:
  0.0 1.4 copy.7.routes_ref
  1.4 135.0 %shard_map.64 = bf16[16,4096]{1,0:T(8,128)(2,1)} custom-call(bf16[16,4096]{1,0:T(8,128)(2,1)} %x_ref.1, s32[16,2]{1,0:T(8,128)} %copy.7.routes_ref, bf16[8,4096]{1,0:T(8,128)(2,1)} %bitcast.7, bf16[4096,896]{1,0:T(8,128)(2,1)} %bitcast.4, bf16[4096,896]{1,0:T(8,128)(2,1)} %bitcast.5, bf16[896,4096]{1,0:T(8,128)(2,1)} %bitcast.6), custom_call_target="tpu_custom_call" | custom-call | flops 22548578304 | bytes 22020096 | tf_op jit(solution)/shard_map/pallas_call | solution.py:333
  136.3 1.6 %copy.9 = bf16[16,4096]{1,0:T(8,128)(2,1)} copy(bf16[16,4096]{1,0:T(8,128)(2,1)} %shard_map.64) | data formatting | bytes 262144

commit v3 on v1

v3 whole, which is shorter than its diff:
```python
import jax
import jax.numpy as jnp
from jax import lax
from jax.experimental import pallas as pl
from jax.experimental.pallas import tpu as pltpu
from jax.sharding import PartitionSpec as P

MESH = pl.DeviceIdType.MESH
F32, BF16 = jnp.float32, jnp.bfloat16
SIDE = 4
WAVES = 2
COLOURS = (((0, 768), (768, 640), (1408, 640)), ((0, 640), (640, 768), (1408, 640)))
LANES = 128
VMEM_BYTES = 64 * 1024 * 1024 - 65536
OFFSETS = (1, -1, 2)


def spread_dims(colour, phase):
    return sorted((colour + j) % 3 for j in range(phase))


def kernel(x_ref, routes_ref, router_ref, wg_ref, wu_ref, wd_ref, out_ref,
           wgu, wd, rows, meta, xs, staging, outgoing, acts, hidden, back, final,
           ra2, rb2, r1, r0,
           w_sem, ag_send, ag_recv, meta_send, meta_recv, swap_send, swap_recv, in_send, in_recv,
           back_send, back_recv, rs_send, rs_recv):
    section, expert = lax.axis_index("section"), lax.axis_index("expert")
    core = lax.rem(expert, 2)
    pos = [lax.div(section, SIDE), lax.div(expert, 2), lax.rem(section, SIDE)]
    tok, width = x_ref.shape
    half_width = width // 2
    ff = wg_ref.shape[1]
    other_expert = pos[1] * 2 + 1 - core
    twin = (section, other_expert)
    my_start = pl.multiple_of(core * half_width, half_width)
    twin_start = pl.multiple_of((1 - core) * half_width, half_width)

    def step(dim, off):
        return lax.rem(pos[dim] + off + SIDE, SIDE)

    def near(dim, off):
        p = list(pos)
        p[dim] = step(dim, off)
        return (p[0] * SIDE + p[2], p[1] * 2 + core)

    loads = [
        pltpu.make_async_copy(wg_ref, wgu.at[:, pl.ds(0, ff)], w_sem.at[0]),
        pltpu.make_async_copy(wu_ref, wgu.at[:, pl.ds(ff, ff)], w_sem.at[1]),
        pltpu.make_async_copy(wd_ref, wd, w_sem.at[2]),
    ]

    barrier = pltpu.get_barrier_semaphore()
    greeted = [near(d, o) for d in range(3) for o in OFFSETS] + [twin]
    for device in greeted:
        pl.semaphore_signal(barrier, inc=1, device_id=device, device_id_type=MESH)
    for load in loads:
        load.start()

    rows[core, pos[0], pos[1], pos[2]] = x_ref[:, pl.ds(my_start, half_width)]

    def send(src, dst, sends, recvs, n, device):
        copy = pltpu.make_async_remote_copy(src_ref=src, dst_ref=dst, send_sem=sends.at[n], recv_sem=recvs.at[n],
                                            device_id=device, device_id_type=MESH)
        copy.start()
        return copy

    pl.semaphore_wait(barrier, len(greeted))
    swap = send(x_ref.at[:, pl.ds(twin_start, half_width)], rows.at[core, pos[0], pos[1], pos[2]],
                swap_send, swap_recv, 0, twin)

    logits = lax.dot_general(x_ref[...], router_ref[...], (((1,), (1,)), ((), ())),
                             preferred_element_type=F32)
    first, second = routes_ref[:, 0:1], routes_ref[:, 1:2]
    narrow = lax.broadcasted_iota(jnp.int32, logits.shape, 1)
    gap = (jnp.sum(jnp.where(narrow == first, logits, 0.0), axis=1, keepdims=True)
           - jnp.sum(jnp.where(narrow == second, logits, 0.0), axis=1, keepdims=True))
    gate0 = jax.nn.sigmoid(gap)
    gate1 = 1.0 - gate0
    lane = lax.broadcasted_iota(jnp.int32, (tok, LANES), 1)
    named = jnp.where(lane == first, 1.0, 0.0) + jnp.where(lane == second, 1.0, 0.0)
    below = jnp.where(lax.broadcasted_iota(jnp.int32, (tok, tok), 0)
                      > lax.broadcasted_iota(jnp.int32, (tok, tok), 1), 1.0, 0.0)
    earlier = jnp.dot(below.astype(BF16), named.astype(BF16), preferred_element_type=F32)
    facts = (named * (earlier + 1.0) + jnp.where(lane == first + 8, gate0, 0.0)
             + jnp.where(lane == second + 8, gate1, 0.0))
    meta[core, pos[0], pos[1], pos[2]] = facts.astype(BF16)

    def piece(wave, colour, phase, at, half):
        start, size = COLOURS[wave][colour]
        index = list(pos)
        index[(colour + phase) % 3] = at
        for n, d in enumerate(spread_dims(colour, phase)):
            index[d] = pl.ds(0, SIDE) if n or half is None else pl.ds(2 * half, 2)
        return rows.at[wave, index[0], index[1], index[2], :, pl.ds(start, size)]

    class Gather:
        def __init__(self, wave):
            self.wave, self.all, self.last = wave, [], []

        def number(self, phase, colour, n):
            return self.wave * 36 + (colour * 3 + n if phase < 2 else 18 + colour * 6 + n) + 9 * (phase == 1)

        def send(self, phase, colour, n, view, off):
            copy = send(view, view, ag_send, ag_recv, self.number(phase, colour, n), near((colour + phase) % 3, off))
            self.all.append(copy)
            return copy

        def arrive(self):
            for copy in self.last:
                copy.wait_recv()

        def direct(self, phase):
            self.arrive()
            self.last = []
            for n, off in enumerate(OFFSETS):
                for colour in range(3):
                    view = piece(self.wave, colour, phase, pos[(colour + phase) % 3], None)
                    self.last.append(self.send(phase, colour, n, view, off))

        def planes(self):
            self.arrive()
            self.last, self.relayed = [], []
            for n, (off, half) in enumerate(((1, 0), (-1, 1), (1, 1), (-1, 0))):
                for colour in range(3):
                    view = piece(self.wave, colour, 2, pos[(colour + 2) % 3], half)
                    copy = self.send(2, colour, n, view, off)
                    (self.relayed if n < 2 else self.last).append((colour, off, half, copy) if n < 2 else copy)

        def relay(self):
            for n, (colour, off, half, copy) in enumerate(self.relayed):
                copy.wait_recv()
                view = piece(self.wave, colour, 2, step((colour + 2) % 3, -off), half)
                self.last.append(self.send(2, colour, 4 + n // 3, view, off))

        def drain(self):
            for copy in self.all:
                copy.wait_send()

    meta_copies = []

    def meta_step(phase):
        for copy in meta_copies[-3:]:
            copy.wait_recv()
        if phase == 3:
            return send(meta.at[core], meta.at[core], meta_send, meta_recv, 9, twin)
        index = [pl.ds(0, SIDE) if d < phase else pos[d] for d in range(3)]
        view = meta.at[core, index[0], index[1], index[2]]
        for n, off in enumerate(OFFSETS):
            meta_copies.append(send(view, view, meta_send, meta_recv, 3 * phase + n, near(phase, off)))

    swap.wait_recv()
    g0, g1 = Gather(0), Gather(1)
    g0.direct(0)
    meta_step(0)
    g1.direct(0)
    g0.direct(1)
    meta_step(1)
    g0.planes()
    meta_step(2)
    g0.relay()
    g1.direct(1)
    meta_swap = meta_step(3)
    g0.arrive()
    meta_swap.wait_recv()

    groups = 8
    span = 64
    wide = lax.broadcasted_iota(jnp.int32, (LANES, LANES), 1)
    tall = lax.broadcasted_iota(jnp.int32, (LANES, LANES), 0)
    block_of = (lax.div(tall, tok) * 8).astype(F32)[:, 0:1]
    wide_f = wide.astype(F32)

    def placing(wave, g, weighted):
        facts = meta[wave, lax.div(g, 2), pl.ds(lax.rem(g, 2) * 2, 2)].reshape(LANES, LANES).astype(F32)
        total = jnp.zeros((LANES, LANES), F32)
        for which, base in ((expert, 0.0), (other_expert, float(span))):
            slot = jnp.sum(jnp.where(wide == which, facts, 0.0), axis=1, keepdims=True)
            place = jnp.where(slot > 0.5, block_of + slot + (base - 1.0), -1.0)
            value = 1.0
            if weighted:
                value = jnp.sum(jnp.where(wide == which + 8, facts, 0.0), axis=1, keepdims=True)
            total = total + jnp.where(wide_f == place, value, 0.0)
        return total.astype(BF16)

    chunk = 1024
    n_tile = 256
    tile = 256
    slots = groups * span

    def pick(wave, part):
        def one(g, carry):
            place = placing(wave, g, False)
            at = pl.ds(pl.multiple_of(g * span, span), span)
            for n in range(half_width // chunk):
                block = rows[wave, lax.div(g, 2), pl.ds(lax.rem(g, 2) * 2, 2), :, :, pl.ds(n * chunk, chunk)]
                got = lax.dot_general(place, block.reshape(LANES, chunk), (((0,), (0,)), ((), ())),
                                      preferred_element_type=F32).astype(BF16)
                xs[wave, at, pl.ds(pl.multiple_of(my_start + n * chunk, chunk), chunk)] = got[:span]
                staging[at, pl.ds(n * chunk, chunk)] = got[span:]
            return carry

        lax.fori_loop(part * 4, part * 4 + 4, one, 0)
        at = pl.ds(part * 256, 256)
        return send(staging.at[at], xs.at[wave, at, pl.ds(my_start, half_width)],
                    in_send, in_recv, wave * 2 + part, twin)

    def up_projection(wave, r):
        def one(n, carry):
            cols = pl.ds(pl.multiple_of(n * n_tile, n_tile), n_tile)
            acts[:, cols] = jnp.dot(xs[wave], wgu[:, cols], preferred_element_type=F32)
            return carry

        lax.fori_loop(0, 2 * ff // n_tile, one, 0)

        def squash(i, carry):
            at = pl.ds(pl.multiple_of(i * 32, 32), 32)
            gate = acts[at, pl.ds(0, ff)]
            hidden[at] = (gate / (1.0 + jnp.exp(-gate)) * acts[at, pl.ds(ff, ff)]).astype(BF16)
            return carry

        lax.fori_loop(0, slots // 32, squash, 0)

    def down_twin(wave, part):
        quarter = half_width // 2

        def one(n, carry):
            at = part * quarter + n * n_tile
            outgoing[:, pl.ds(pl.multiple_of(at, n_tile), n_tile)] = jnp.dot(
                hidden[...], wd[:, pl.ds(pl.multiple_of(twin_start + at, n_tile), n_tile)],
                preferred_element_type=F32).astype(BF16)
            return carry

        lax.fori_loop(0, quarter // n_tile, one, 0)
        cols = pl.ds(part * quarter, quarter)
        return send(outgoing.at[:, cols], back.at[wave, :, cols], back_send, back_recv, wave * 2 + part, twin)

    def down_mine(wave):
        def one(n, carry):
            at = n * n_tile
            xs[wave, :, pl.ds(pl.multiple_of(at, n_tile), n_tile)] = jnp.dot(
                hidden[...], wd[:, pl.ds(pl.multiple_of(my_start + at, n_tile), n_tile)],
                preferred_element_type=F32).astype(BF16)
            return carry

        lax.fori_loop(0, half_width // n_tile, one, 0)

    def mix(wave):
        def one(g, carry):
            place = placing(wave, g, True)
            at = pl.ds(pl.multiple_of(g * span, span), span)
            for n in range(half_width // chunk):
                cols = pl.ds(n * chunk, chunk)
                both = jnp.concatenate([xs[wave, at, cols], back[wave, at, cols]], axis=0)
                got = jnp.dot(place, both, preferred_element_type=F32).astype(BF16)
                rows[wave, lax.div(g, 2), pl.ds(lax.rem(g, 2) * 2, 2), :, :, cols] = got.reshape(2, SIDE, tok, chunk)
            return carry

        lax.fori_loop(0, groups, one, 0)

    class Scatter:
        def __init__(self, wave):
            self.wave, self.all = wave, []

        def send(self, phase, colour, n, view, landing, off):
            number = self.wave * 36 + (18 + colour * 6 + n if phase == 2 else 9 * phase + colour * 3 + n)
            copy = send(view, landing, rs_send, rs_recv, number, near((colour + phase) % 3, off))
            self.all.append(copy)
            return copy

        def land(self, ref, colour, phase, way, half):
            cols = pl.ds(*COLOURS[self.wave][colour])
            if phase == 0:
                return ref.at[self.wave, way, :, cols]
            lead = pl.ds(0, ref.shape[2]) if half is None else pl.ds(2 * half, 2)
            if phase == 1:
                return ref.at[self.wave, way, lead, :, cols]
            return ref.at[self.wave, way, lead, :, :, cols]

        def add(self, colour, phase, at, half, ref, ways):
            cols = pl.ds(*COLOURS[self.wave][colour])
            dims = spread_dims(colour, phase)

            def one(i, carry):
                index = list(pos)
                index[(colour + phase) % 3] = at
                lead, low = (lax.div(i, SIDE), lax.rem(i, SIDE)) if phase == 2 else (i, None)
                if phase == 2:
                    index[dims[1]] = low
                if phase >= 1:
                    index[dims[0]] = lead if half is None else lead + 2 * half
                here = (self.wave, index[0], index[1], index[2], slice(None), cols)
                total = rows[here].astype(F32)
                for way in ways:
                    where = {0: (way,), 1: (way, lead), 2: (way, lead, low)}[phase]
                    total = total + ref[(self.wave,) + where + (slice(None), cols)].astype(F32)
                rows[here] = total.astype(BF16)
                return carry

            count = (SIDE if half is None else 2) if phase >= 1 else 1
            lax.fori_loop(0, count * SIDE if phase == 2 else count, one, 0)

        def planes(self):
            self.fars, self.seconds = [], []
            for n, (off, half) in enumerate(((1, 0), (-1, 1))):
                for colour in range(3):
                    at = step((colour + 2) % 3, 2)
                    self.fars.append((colour, off, half, n, self.send(
                        2, colour, n, piece(self.wave, colour, 2, at, half),
                        self.land(ra2, colour, 2, n, None), off)))
            for n, (off, half) in enumerate(((1, 1), (-1, 0))):
                for colour in range(3):
                    at = step((colour + 2) % 3, off)
                    self.seconds.append(self.send(
                        2, colour, 2 + n, piece(self.wave, colour, 2, at, half),
                        self.land(rb2, colour, 2, n, half), off))

        def relay(self):
            for colour, off, half, n, copy in self.fars:
                copy.wait_recv()
                at = step((colour + 2) % 3, off)
                self.add(colour, 2, at, half, ra2, (n,))
                self.seconds.append(self.send(2, colour, 4 + n, piece(self.wave, colour, 2, at, half),
                                              self.land(rb2, colour, 2, n, half), off))

        def own_plane(self):
            for copy in self.seconds:
                copy.wait_recv()
            for colour in range(3):
                self.add(colour, 2, pos[(colour + 2) % 3], None, rb2, (0, 1))

        def direct(self, phase):
            ref = r1 if phase == 1 else r0
            self.last = []
            for n, off in ((2, 2), (0, 1), (1, -1)):
                for colour in range(3):
                    at = step((colour + phase) % 3, off)
                    self.last.append(self.send(phase, colour, n, piece(self.wave, colour, phase, at, None),
                                               self.land(ref, colour, phase, n, None), off))

        def settle(self, phase):
            ref = r1 if phase == 1 else r0
            for copy in self.last:
                copy.wait_recv()
            for colour in range(3):
                self.add(colour, phase, pos[(colour + phase) % 3], None, ref, (0, 1, 2))

        def drain(self):
            for copy in self.all:
                copy.wait_send()

    picked0 = [pick(0, 0)]
    g1.planes()
    picked0.append(pick(0, 1))
    loads[0].wait()
    loads[1].wait()
    for copy in picked0:
        copy.wait()
    up_projection(0, 0)
    g1.relay()
    loads[2].wait()
    sent0 = [down_twin(0, 0), down_twin(0, 1)]
    down_mine(0)
    g0.drain()
    for copy in sent0:
        copy.wait()
    mix(0)
    s0, s1 = Scatter(0), Scatter(1)
    s0.planes()
    g1.arrive()
    picked1 = [pick(1, 0), pick(1, 1)]
    s0.relay()
    for copy in picked1:
        copy.wait()
    up_projection(1, 0)
    sent1 = [down_twin(1, 0), down_twin(1, 1)]
    s0.own_plane()
    s0.direct(1)
    down_mine(1)
    g1.drain()
    for copy in sent1:
        copy.wait()
    mix(1)
    s1.planes()
    s0.settle(1)
    s0.direct(0)
    s1.relay()
    s0.settle(0)
    s1.own_plane()
    s1.direct(1)
    s1.settle(1)
    s1.direct(0)
    s1.settle(0)
    swap.wait_send()
    ending = send(rows.at[1 - core, pos[0], pos[1], pos[2]], final, swap_send, swap_recv, 1, twin)
    out_ref[:, pl.ds(my_start, half_width)] = rows[core, pos[0], pos[1], pos[2]]
    for copy in meta_copies + [meta_swap]:
        copy.wait_send()
    s0.drain()
    s1.drain()
    ending.wait()
    out_ref[:, pl.ds(twin_start, half_width)] = final[...]


def shards(tokens, routes, router_weight, gate_weight, up_weight, down_weight):
    tok, width = tokens.shape
    half = width // 2
    ff = gate_weight.shape[2]
    cube = (WAVES, SIDE, SIDE, SIDE)
    vmem = pl.BlockSpec(memory_space=pltpu.VMEM)
    anywhere = pl.BlockSpec(memory_space=pl.ANY)
    dma = pltpu.SemaphoreType.DMA
    return pl.pallas_call(
        kernel,
        out_shape=jax.ShapeDtypeStruct((tok, width), BF16),
        in_specs=[vmem, vmem, vmem, anywhere, anywhere, anywhere],
        out_specs=vmem,
        scratch_shapes=[
            pltpu.VMEM((width, 2 * ff), BF16),
            pltpu.VMEM((ff, width), BF16),
            pltpu.VMEM(cube + (tok, half), BF16),
            pltpu.VMEM(cube + (tok, LANES), BF16),
            pltpu.VMEM((WAVES, 512, width), BF16),
            pltpu.VMEM((512, half), BF16),
            pltpu.VMEM((512, half), BF16),
            pltpu.VMEM((512, 2 * ff), F32),
            pltpu.VMEM((512, ff), BF16),
            pltpu.VMEM((WAVES, 512, half), BF16),
            pltpu.VMEM((tok, half), BF16),
            pltpu.VMEM((WAVES, 2, 2, SIDE, tok, half), BF16),
            pltpu.VMEM((WAVES, 2, SIDE, SIDE, tok, half), BF16),
            pltpu.VMEM((WAVES, 3, SIDE, tok, half), BF16),
            pltpu.VMEM((WAVES, 3, tok, half), BF16),
            dma((3,)),
            dma((72,)), dma((72,)),
            dma((10,)), dma((10,)),
            dma((2,)), dma((2,)),
            dma((4,)), dma((4,)),
            dma((4,)), dma((4,)),
            dma((72,)), dma((72,)),
        ],
        compiler_params=pltpu.CompilerParams(
            collective_id=0, has_side_effects=True, vmem_limit_bytes=VMEM_BYTES
        ),
        cost_estimate=pl.CostEstimate(flops=2 * 3 * 1024 * width * ff, bytes_accessed=6 * ff * width,
                                      transcendentals=1024 * ff),
    )(tokens, routes, router_weight.T, gate_weight[0], up_weight[0], down_weight[0])


def solution(mesh):
    in_specs = (
        P(("section", "expert"), None),
        P(("section", "expert"), None),
        P(),
        P("expert", None, "section"),
        P("expert", None, "section"),
        P("expert", "section", None),
    )
    out_specs = P(("section", "expert"), None)
    return jax.shard_map(shards, mesh=mesh, in_specs=in_specs, out_specs=out_specs, check_vma=False)
```

time: 241 us -> 129 us (0.54)
  waiting for transfers between devices: 156 us -> 0 us
  Pallas kernels: 0 us -> 125 us
  matrix products: 37.9 us -> 0 us
  blocking collectives: 29.6 us -> 0 us
  between operations: 13.5 us -> 0.01 us
    pallas_call x0 -> x1, Pallas kernels: none -> 125 us  [shards(): pl.pallas_call(kernel, out_shape=jax.ShapeDtypeStruct((tok, width), BF16)...]
    reduce_scatter x1 -> x0, waiting for transfers between devices: 84.9 us -> none  [shards(): lax.psum_scatter(partial_sum, 'section', scatter_dimension=0, tiled=True)]
    all_gather x1 -> x0, waiting for transfers between devices: 71.3 us -> none  [shards(): rows = lax.all_gather(arrived, 'section', axis=0, tiled=True)]
    dot_general x6 -> x0, matrix products: 37.9 us -> none  [the longest x1 12.5 us: shards(): up_act = jnp.dot(rows, up_weight[0], preferred_element_type=jnp.float32)]
    all_to_all x2 -> x0, blocking collectives: 29.6 us -> none  [the longest x1 14.8 us: shards(): lax.all_to_all(outgoing, 'expert', split_axis=0, concat_axis=0, tiled=True)]
  transfers between devices with their start and end apart: 2 -> 0, of which waited for: 2 -> 0; matrix products, arithmetic and copies ran while one was open for 0% -> 0% of each run, Pallas kernels for 0% -> 0%
where the time goes in v3:
time: 129 us; the launch traced here: 128 us
  Pallas kernels  125 us (97%)
  local copies, waits for them, and re-layouts  2.92 us (2%)
    pallas_call x1, Pallas kernels, shards(): pl.pallas_call(kernel, out_shape=jax.ShapeDtypeStruct((tok, width), BF16)...  125 us
    unnamed x2, local copies, waits for them, and re-layouts  2.92 us

profile of v3, /device:TPU:0, one launch (start us, length us, event | category | flops | bytes accessed | tf_op | source)
XLA Modules:
  0.0 127.7 jit_solution(6858442356032000435)
XLA Ops:
  0.0 1.4 %copy.7.routes_ref = s32[16,2]{1,0:T(8,128)} copy(s32[16,2]{0,1:T(2,128)} %param.7) | data formatting | bytes 256 | tf_op args[1]
  1.4 124.8 %shard_map.64 = bf16[16,4096]{1,0:T(8,128)(2,1)} custom-call(bf16[16,4096]{1,0:T(8,128)(2,1)} %x_ref.1, s32[16,2]{1,0:T(8,128)} %copy.7.routes_ref, bf16[8,4096]{1,0:T(8,128)(2,1)} %bitcast.7, bf16[4096,896]{1,0:T(8,128)(2,1)} %bitcast.4, bf16[4096,896]{1,0:T(8,128)(2,1)} %bitcast.5, bf16[896,4096]{1,0:T(8,128)(2,1)} %bitcast.6), custom_call_target="tpu_custom_call" | custom-call | flops 22548578304 | bytes 22020096 | tf_op jit(solution)/shard_map/pallas_call | solution.py:412
  126.1 1.6 %copy.9 = bf16[16,4096]{1,0:T(8,128)(2,1)} copy(bf16[16,4096]{1,0:T(8,128)(2,1)} %shard_map.64) | data formatting | bytes 262144

commit v4 on v3

v4 whole, which is shorter than its diff:
```python
import jax
import jax.numpy as jnp
from jax import lax
from jax.experimental import pallas as pl
from jax.experimental.pallas import tpu as pltpu
from jax.sharding import PartitionSpec as P

MESH = pl.DeviceIdType.MESH
F32, BF16 = jnp.float32, jnp.bfloat16
SIDE = 4
WAVES = 2
FORTH = ((0, 768), (768, 768), (1536, 640))
BACK = ((0, 768), (768, 640), (1408, 640))
LANES = 128
VMEM_BYTES = 64 * 1024 * 1024 - 65536
OFFSETS = (1, -1, 2)


def spread_dims(colour, phase):
    return sorted((colour + j) % 3 for j in range(phase))


def kernel(x_ref, routes_ref, router_ref, wg_ref, wu_ref, wd_ref, out_ref,
           wgu, wd, rows, places, xs, staging, outgoing, acts, hidden, back, final,
           ra2, rb2, r1, r0,
           w_sem, ag_send, ag_recv, swap_send, swap_recv, in_send, in_recv,
           back_send, back_recv, rs_send, rs_recv):
    section, expert = lax.axis_index("section"), lax.axis_index("expert")
    core = lax.rem(expert, 2)
    pos = [lax.div(section, SIDE), lax.div(expert, 2), lax.rem(section, SIDE)]
    tok, width = x_ref.shape
    half_width = width // 2
    ff = wg_ref.shape[1]
    other_expert = pos[1] * 2 + 1 - core
    twin = (section, other_expert)
    my_start = pl.multiple_of(core * half_width, half_width)
    twin_start = pl.multiple_of((1 - core) * half_width, half_width)

    def step(dim, off):
        return lax.rem(pos[dim] + off + SIDE, SIDE)

    def near(dim, off):
        p = list(pos)
        p[dim] = step(dim, off)
        return (p[0] * SIDE + p[2], p[1] * 2 + core)

    loads = [
        pltpu.make_async_copy(wg_ref, wgu.at[:, pl.ds(0, ff)], w_sem.at[0]),
        pltpu.make_async_copy(wu_ref, wgu.at[:, pl.ds(ff, ff)], w_sem.at[1]),
        pltpu.make_async_copy(wd_ref, wd, w_sem.at[2]),
    ]

    barrier = pltpu.get_barrier_semaphore()
    greeted = [near(d, o) for d in range(3) for o in OFFSETS] + [twin]
    for device in greeted:
        pl.semaphore_signal(barrier, inc=1, device_id=device, device_id_type=MESH)
    for load in loads:
        load.start()

    body = pl.ds(0, half_width)
    tail = pl.ds(half_width, LANES)
    rows[core, pos[0], pos[1], pos[2], :, body] = x_ref[:, pl.ds(my_start, half_width)]

    logits = lax.dot_general(x_ref[...], router_ref[...], (((1,), (1,)), ((), ())),
                             preferred_element_type=F32)
    square = (tok, tok)
    down_rows, over_lanes = lax.broadcasted_iota(jnp.int32, square, 0), lax.broadcasted_iota(jnp.int32, square, 1)

    def upright(k):
        spread = jnp.broadcast_to(routes_ref[k:k + 1, :], square)
        return jnp.sum(jnp.where(down_rows == over_lanes, spread, 0), axis=1, keepdims=True)

    first, second = upright(0), upright(1)
    narrow = lax.broadcasted_iota(jnp.int32, logits.shape, 1)
    gap = (jnp.sum(jnp.where(narrow == first, logits, 0.0), axis=1, keepdims=True)
           - jnp.sum(jnp.where(narrow == second, logits, 0.0), axis=1, keepdims=True))
    gate0 = jax.nn.sigmoid(gap)
    gate1 = 1.0 - gate0
    lane = lax.broadcasted_iota(jnp.int32, (tok, LANES), 1)
    named = jnp.where(lane == first, 1.0, 0.0) + jnp.where(lane == second, 1.0, 0.0)
    below = jnp.where(down_rows > over_lanes, 1.0, 0.0)
    earlier = jnp.dot(below.astype(BF16), named.astype(BF16), preferred_element_type=F32)
    facts = (named * (earlier + 1.0) + jnp.where(lane == first + 8, gate0, 0.0)
             + jnp.where(lane == second + 8, gate1, 0.0))
    rows[core, pos[0], pos[1], pos[2], :, tail] = facts.astype(BF16)

    def send(src, dst, sends, recvs, n, device):
        copy = pltpu.make_async_remote_copy(src_ref=src, dst_ref=dst, send_sem=sends.at[n], recv_sem=recvs.at[n],
                                            device_id=device, device_id_type=MESH)
        copy.start()
        return copy

    pl.semaphore_wait(barrier, len(greeted))
    swap = send(x_ref.at[:, pl.ds(twin_start, half_width)], rows.at[core, pos[0], pos[1], pos[2], :, body],
                swap_send, swap_recv, 0, twin)

    own_facts = rows.at[core, pos[0], pos[1], pos[2], :, tail]
    swap_facts = send(own_facts, own_facts, swap_send, swap_recv, 2, twin)

    def piece(wave, colour, phase, at, half, colours):
        start, size = colours[colour]
        index = list(pos)
        index[(colour + phase) % 3] = at
        for n, d in enumerate(spread_dims(colour, phase)):
            index[d] = pl.ds(0, SIDE) if n or half is None else pl.ds(2 * half, 2)
        return rows.at[wave, index[0], index[1], index[2], :, pl.ds(start, size)]

    class Gather:
        def __init__(self, wave):
            self.wave, self.all, self.last = wave, [], []

        def number(self, phase, colour, n):
            return self.wave * 36 + (colour * 3 + n if phase < 2 else 18 + colour * 6 + n) + 9 * (phase == 1)

        def send(self, phase, colour, n, view, off):
            copy = send(view, view, ag_send, ag_recv, self.number(phase, colour, n), near((colour + phase) % 3, off))
            self.all.append(copy)
            return copy

        def arrive(self):
            for copy in self.last:
                copy.wait_recv()

        def direct(self, phase):
            self.arrive()
            self.last = []
            for n, off in enumerate(OFFSETS):
                for colour in range(3):
                    view = piece(self.wave, colour, phase, pos[(colour + phase) % 3], None, FORTH)
                    self.last.append(self.send(phase, colour, n, view, off))

        def planes(self):
            self.arrive()
            self.last, self.relayed = [], []
            for n, (off, half) in enumerate(((1, 0), (-1, 1), (1, 1), (-1, 0))):
                for colour in range(3):
                    view = piece(self.wave, colour, 2, pos[(colour + 2) % 3], half, FORTH)
                    copy = self.send(2, colour, n, view, off)
                    (self.relayed if n < 2 else self.last).append((colour, off, half, copy) if n < 2 else copy)

        def relay(self):
            for n, (colour, off, half, copy) in enumerate(self.relayed):
                copy.wait_recv()
                view = piece(self.wave, colour, 2, step((colour + 2) % 3, -off), half, FORTH)
                self.last.append(self.send(2, colour, 4 + n // 3, view, off))

        def drain(self):
            for copy in self.all:
                copy.wait_send()

    swap.wait_recv()
    swap_facts.wait_recv()
    g0, g1 = Gather(0), Gather(1)
    g0.direct(0)
    g1.direct(0)
    g0.direct(1)
    g1.direct(1)
    g0.planes()
    g0.relay()
    g0.arrive()

    groups = 8
    span = 64
    wide = lax.broadcasted_iota(jnp.int32, (LANES, LANES), 1)
    tall = lax.broadcasted_iota(jnp.int32, (LANES, LANES), 0)
    block_of = (lax.div(tall, tok) * 8).astype(F32)[:, 0:1]
    wide_f = wide.astype(F32)

    def placing(wave, g):
        facts = rows[wave, lax.div(g, 2), pl.ds(lax.rem(g, 2) * 2, 2), :, :, tail].reshape(LANES, LANES).astype(F32)
        plain = jnp.zeros((LANES, LANES), F32)
        weighted = jnp.zeros((LANES, LANES), F32)
        for which, base in ((expert, 0.0), (other_expert, float(span))):
            slot = jnp.sum(jnp.where(wide == which, facts, 0.0), axis=1, keepdims=True)
            gate = jnp.sum(jnp.where(wide == which + 8, facts, 0.0), axis=1, keepdims=True)
            hit = wide_f == jnp.where(slot > 0.5, block_of + slot + (base - 1.0), -1.0)
            plain = jnp.where(hit, 1.0, plain)
            weighted = jnp.where(hit, gate, weighted)
        places[wave, g] = weighted.astype(BF16)
        return plain.astype(BF16)

    chunk = 1024
    n_tile = 256
    tile = 256
    slots = groups * span

    def pick(wave, part):
        def one(g, carry):
            place = placing(wave, g)
            at = pl.ds(pl.multiple_of(g * span, span), span)
            for n in range(half_width // chunk):
                block = rows[wave, lax.div(g, 2), pl.ds(lax.rem(g, 2) * 2, 2), :, :, pl.ds(n * chunk, chunk)]
                got = lax.dot_general(place, block.reshape(LANES, chunk), (((0,), (0,)), ((), ())),
                                      preferred_element_type=F32).astype(BF16)
                xs[wave, at, pl.ds(pl.multiple_of(my_start + n * chunk, chunk), chunk)] = got[:span]
                staging[at, pl.ds(n * chunk, chunk)] = got[span:]
            return carry

        lax.fori_loop(part * 4, part * 4 + 4, one, 0)
        at = pl.ds(part * 256, 256)
        return send(staging.at[at], xs.at[wave, at, pl.ds(my_start, half_width)],
                    in_send, in_recv, wave * 2 + part, twin)

    def up_projection(wave, first, count):
        at = pl.ds(first, count)

        def one(n, carry):
            cols = pl.ds(pl.multiple_of(n * n_tile, n_tile), n_tile)
            acts[at, cols] = jnp.dot(xs[wave, at], wgu[:, cols], preferred_element_type=F32)
            return carry

        lax.fori_loop(0, 2 * ff // n_tile, one, 0)

    def activate():
        def squash(i, carry):
            at = pl.ds(pl.multiple_of(i * 32, 32), 32)
            gate = acts[at, pl.ds(0, ff)]
            hidden[at] = (gate / (1.0 + jnp.exp(-gate)) * acts[at, pl.ds(ff, ff)]).astype(BF16)
            return carry

        lax.fori_loop(0, slots // 32, squash, 0)

    def down_twin(wave, part):
        quarter = half_width // 2

        def one(n, carry):
            at = part * quarter + n * n_tile
            outgoing[:, pl.ds(pl.multiple_of(at, n_tile), n_tile)] = jnp.dot(
                hidden[...], wd[:, pl.ds(pl.multiple_of(twin_start + at, n_tile), n_tile)],
                preferred_element_type=F32).astype(BF16)
            return carry

        lax.fori_loop(0, quarter // n_tile, one, 0, unroll=4)
        cols = pl.ds(part * quarter, quarter)
        return send(outgoing.at[:, cols], back.at[wave, :, cols], back_send, back_recv, wave * 2 + part, twin)

    def down_mine(wave):
        def one(n, carry):
            at = n * n_tile
            xs[wave, :, pl.ds(pl.multiple_of(at, n_tile), n_tile)] = jnp.dot(
                hidden[...], wd[:, pl.ds(pl.multiple_of(my_start + at, n_tile), n_tile)],
                preferred_element_type=F32).astype(BF16)
            return carry

        lax.fori_loop(0, half_width // n_tile, one, 0, unroll=4)

    def mix(wave, colour):
        start, size = BACK[colour]
        cols = pl.ds(start, size)

        def one(g, carry):
            at = pl.ds(g * span, span)
            both = jnp.concatenate([xs[wave, at, cols], back[wave, at, cols]], axis=0)
            got = jnp.dot(places[wave, g], both, preferred_element_type=F32).astype(BF16)
            rows[wave, g // 2, pl.ds(g % 2 * 2, 2), :, :, cols] = got.reshape(2, SIDE, tok, size)
            return carry

        for g in range(groups):
            one(g, 0)

    class Scatter:
        def __init__(self, wave):
            self.wave, self.all, self.fars, self.seconds = wave, [], [], []

        def send(self, phase, colour, n, view, landing, off):
            number = self.wave * 36 + (18 + colour * 6 + n if phase == 2 else 9 * phase + colour * 3 + n)
            copy = send(view, landing, rs_send, rs_recv, number, near((colour + phase) % 3, off))
            self.all.append(copy)
            return copy

        def land(self, ref, colour, phase, way, half):
            cols = pl.ds(*BACK[colour])
            if phase == 0:
                return ref.at[self.wave, way, :, cols]
            lead = pl.ds(0, ref.shape[2]) if half is None else pl.ds(2 * half, 2)
            if phase == 1:
                return ref.at[self.wave, way, lead, :, cols]
            return ref.at[self.wave, way, lead, :, :, cols]

        def add(self, colour, phase, at, half, ref, ways):
            cols = pl.ds(*BACK[colour])
            dims = spread_dims(colour, phase)

            def one(lead, carry):
                index = list(pos)
                index[(colour + phase) % 3] = at
                if phase == 2:
                    index[dims[1]] = pl.ds(0, SIDE)
                    index[dims[0]] = lead if half is None else lead + 2 * half
                if phase == 1:
                    index[dims[0]] = pl.ds(0, SIDE)
                here = (self.wave, index[0], index[1], index[2], slice(None), cols)
                total = rows[here].astype(F32)
                for way in ways:
                    where = (self.wave, way) + {0: (), 1: (pl.ds(0, SIDE),), 2: (lead, pl.ds(0, SIDE))}[phase]
                    total = total + ref[where + (slice(None), cols)].astype(F32)
                rows[here] = total.astype(BF16)
                return carry

            if phase == 2:
                lax.fori_loop(0, SIDE if half is None else 2, one, 0)
            else:
                one(0, 0)

        def planes(self, colour):
            for n, (off, half) in enumerate(((1, 0), (-1, 1))):
                at = step((colour + 2) % 3, 2)
                self.fars.append((colour, off, half, n, self.send(
                    2, colour, n, piece(self.wave, colour, 2, at, half, BACK),
                    self.land(ra2, colour, 2, n, None), off)))
            for n, (off, half) in enumerate(((1, 1), (-1, 0))):
                at = step((colour + 2) % 3, off)
                self.seconds.append(self.send(
                    2, colour, 2 + n, piece(self.wave, colour, 2, at, half, BACK),
                    self.land(rb2, colour, 2, n, half), off))

        def relay(self):
            for colour, off, half, n, copy in self.fars:
                copy.wait_recv()
                at = step((colour + 2) % 3, off)
                self.add(colour, 2, at, half, ra2, (n,))
                self.seconds.append(self.send(2, colour, 4 + n, piece(self.wave, colour, 2, at, half, BACK),
                                              self.land(rb2, colour, 2, n, half), off))

        def own_plane(self):
            for copy in self.seconds:
                copy.wait_recv()
            for colour in range(3):
                self.add(colour, 2, pos[(colour + 2) % 3], None, rb2, (0, 1))

        def direct(self, phase):
            ref = r1 if phase == 1 else r0
            self.last = []
            for n, off in ((2, 2), (0, 1), (1, -1)):
                for colour in range(3):
                    at = step((colour + phase) % 3, off)
                    self.last.append(self.send(phase, colour, n, piece(self.wave, colour, phase, at, None, BACK),
                                               self.land(ref, colour, phase, n, None), off))

        def settle(self, phase):
            ref = r1 if phase == 1 else r0
            for copy in self.last:
                copy.wait_recv()
            for colour in range(3):
                self.add(colour, phase, pos[(colour + phase) % 3], None, ref, (0, 1, 2))

        def drain(self):
            for copy in self.all:
                copy.wait_send()

    picked0 = [pick(0, 0)]
    g1.planes()
    picked0.append(pick(0, 1))
    loads[0].wait()
    loads[1].wait()
    picked0[0].wait()
    up_projection(0, 0, slots // 2)
    g1.relay()
    picked0[1].wait()
    up_projection(0, slots // 2, slots // 2)
    activate()
    loads[2].wait()
    sent0 = [down_twin(0, 0), down_twin(0, 1)]
    down_mine(0)
    g0.drain()
    for copy in sent0:
        copy.wait()
    s0, s1 = Scatter(0), Scatter(1)
    for colour in range(3):
        mix(0, colour)
        s0.planes(colour)
    g1.arrive()
    picked1 = [pick(1, 0), pick(1, 1)]
    picked1[0].wait()
    up_projection(1, 0, slots // 2)
    s0.relay()
    picked1[1].wait()
    up_projection(1, slots // 2, slots // 2)
    activate()
    sent1 = [down_twin(1, 0), down_twin(1, 1)]
    down_mine(1)
    s0.own_plane()
    s0.direct(1)
    g1.drain()
    for copy in sent1:
        copy.wait()
    for colour in range(3):
        mix(1, colour)
        s1.planes(colour)
    s0.settle(1)
    s0.direct(0)
    s1.relay()
    s0.settle(0)
    s1.own_plane()
    s1.direct(1)
    s1.settle(1)
    s1.direct(0)
    s1.settle(0)
    swap.wait_send()
    swap_facts.wait_send()
    ending = send(rows.at[1 - core, pos[0], pos[1], pos[2], :, body], final, swap_send, swap_recv, 1, twin)
    out_ref[:, pl.ds(my_start, half_width)] = rows[core, pos[0], pos[1], pos[2], :, body]
    s0.drain()
    s1.drain()
    ending.wait()
    out_ref[:, pl.ds(twin_start, half_width)] = final[...]


def shards(tokens, routes, router_weight, gate_weight, up_weight, down_weight):
    tok, width = tokens.shape
    half = width // 2
    ff = gate_weight.shape[2]
    cube = (WAVES, SIDE, SIDE, SIDE)
    vmem = pl.BlockSpec(memory_space=pltpu.VMEM)
    anywhere = pl.BlockSpec(memory_space=pl.ANY)
    dma = pltpu.SemaphoreType.DMA
    return pl.pallas_call(
        kernel,
        out_shape=jax.ShapeDtypeStruct((tok, width), BF16),
        in_specs=[vmem, vmem, vmem, anywhere, anywhere, anywhere],
        out_specs=vmem,
        scratch_shapes=[
            pltpu.VMEM((width, 2 * ff), BF16),
            pltpu.VMEM((ff, width), BF16),
            pltpu.VMEM(cube + (tok, half + LANES), BF16),
            pltpu.VMEM((WAVES, 8, LANES, LANES), BF16),
            pltpu.VMEM((WAVES, 512, width), BF16),
            pltpu.VMEM((512, half), BF16),
            pltpu.VMEM((512, half), BF16),
            pltpu.VMEM((512, 2 * ff), F32),
            pltpu.VMEM((512, ff), BF16),
            pltpu.VMEM((WAVES, 512, half), BF16),
            pltpu.VMEM((tok, half), BF16),
            pltpu.VMEM((WAVES, 2, 2, SIDE, tok, half), BF16),
            pltpu.VMEM((WAVES, 2, SIDE, SIDE, tok, half), BF16),
            pltpu.VMEM((WAVES, 3, SIDE, tok, half), BF16),
            pltpu.VMEM((WAVES, 3, tok, half), BF16),
            dma((3,)),
            dma((72,)), dma((72,)),
            dma((3,)), dma((3,)),
            dma((4,)), dma((4,)),
            dma((4,)), dma((4,)),
            dma((72,)), dma((72,)),
        ],
        compiler_params=pltpu.CompilerParams(
            collective_id=0, has_side_effects=True, vmem_limit_bytes=VMEM_BYTES
        ),
        cost_estimate=pl.CostEstimate(flops=2 * 3 * 1024 * width * ff, bytes_accessed=6 * ff * width,
                                      transcendentals=1024 * ff),
    )(tokens, routes.T, router_weight.T, gate_weight[0], up_weight[0], down_weight[0])


def solution(mesh):
    in_specs = (
        P(("section", "expert"), None),
        P(("section", "expert"), None),
        P(),
        P("expert", None, "section"),
        P("expert", None, "section"),
        P("expert", "section", None),
    )
    out_specs = P(("section", "expert"), None)
    return jax.shard_map(shards, mesh=mesh, in_specs=in_specs, out_specs=out_specs, check_vma=False)
```

time: 129 us -> 118 us (0.915)
  Pallas kernels: 125 us -> 115 us
  local copies, waits for them, and re-layouts: 2.92 us -> 1.57 us
    pallas_call x1, Pallas kernels: 125 us -> 115 us  [shards(): pl.pallas_call(kernel, out_shape=jax.ShapeDtypeStruct((tok, width), BF16)...]
    unnamed x2 -> x1, local copies, waits for them, and re-layouts: 2.92 us -> 1.57 us
where the time goes in v4:
time: 118 us; the launch traced here: 116 us
  Pallas kernels  115 us (97%)
  local copies, waits for them, and re-layouts  1.57 us (1%)
    pallas_call x1, Pallas kernels, shards(): pl.pallas_call(kernel, out_shape=jax.ShapeDtypeStruct((tok, width), BF16)...  115 us

profile of v4, /device:TPU:0, one launch (start us, length us, event | category | flops | bytes accessed | tf_op | source)
XLA Modules:
  0.0 116.5 jit_solution(13648759388430623731)
XLA Ops:
  0.0 114.9 %shard_map.64 = bf16[16,4096]{1,0:T(8,128)(2,1)} custom-call(bf16[16,4096]{1,0:T(8,128)(2,1)} %x_ref.1, s32[2,16]{1,0:T(2,128)} %bitcast.9, bf16[8,4096]{1,0:T(8,128)(2,1)} %bitcast.8, bf16[4096,896]{1,0:T(8,128)(2,1)} %bitcast.5, bf16[4096,896]{1,0:T(8,128)(2,1)} %bitcast.6, bf16[896,4096]{1,0:T(8,128)(2,1)} %bitcast.7), custom_call_target="tpu_custom_call" | custom-call | flops 22548578304 | bytes 22020096 | tf_op jit(solution)/shard_map/pallas_call | solution.py:417
  114.9 1.6 %copy.8 = bf16[16,4096]{1,0:T(8,128)(2,1)} copy(bf16[16,4096]{1,0:T(8,128)(2,1)} %shard_map.64) | data formatting | bytes 262144

commit v5 on v4

--- a/solution.py
+++ b/solution.py
@@ -181,6 +181,7 @@
 
     chunk = 1024
     n_tile = 256
+    up_tile = 896
     tile = 256
     slots = groups * span
 
@@ -201,15 +202,16 @@
         return send(staging.at[at], xs.at[wave, at, pl.ds(my_start, half_width)],
                     in_send, in_recv, wave * 2 + part, twin)
 
-    def up_projection(wave, first, count):
-        at = pl.ds(first, count)
+    def up_projection(wave, start, fresh):
+        deep = pl.ds(start, half_width)
 
         def one(n, carry):
-            cols = pl.ds(pl.multiple_of(n * n_tile, n_tile), n_tile)
-            acts[at, cols] = jnp.dot(xs[wave, at], wgu[:, cols], preferred_element_type=F32)
-            return carry
-
-        lax.fori_loop(0, 2 * ff // n_tile, one, 0)
+            cols = pl.ds(pl.multiple_of(n * up_tile, LANES), up_tile)
+            part = jnp.dot(xs[wave, :, deep], wgu[deep, cols], preferred_element_type=F32)
+            acts[:, cols] = part if fresh else acts[:, cols] + part
+            return carry
+
+        lax.fori_loop(0, 2 * ff // up_tile, one, 0)
 
     def activate():
         def squash(i, carry):
@@ -310,39 +312,52 @@
                     self.land(ra2, colour, 2, n, None), off)))
             for n, (off, half) in enumerate(((1, 1), (-1, 0))):
                 at = step((colour + 2) % 3, off)
-                self.seconds.append(self.send(
+                self.seconds.append((colour, self.send(
                     2, colour, 2 + n, piece(self.wave, colour, 2, at, half, BACK),
-                    self.land(rb2, colour, 2, n, half), off))
+                    self.land(rb2, colour, 2, n, half), off)))
 
         def relay(self):
             for colour, off, half, n, copy in self.fars:
                 copy.wait_recv()
                 at = step((colour + 2) % 3, off)
                 self.add(colour, 2, at, half, ra2, (n,))
-                self.seconds.append(self.send(2, colour, 4 + n, piece(self.wave, colour, 2, at, half, BACK),
-                                              self.land(rb2, colour, 2, n, half), off))
-
-        def own_plane(self):
-            for copy in self.seconds:
-                copy.wait_recv()
-            for colour in range(3):
+                self.seconds.append((colour, self.send(
+                    2, colour, 4 + n, piece(self.wave, colour, 2, at, half, BACK),
+                    self.land(rb2, colour, 2, n, half), off)))
+
+        def lines(self):
+            self.last = []
+            for colour in (2, 1, 0):
+                for copy in self.seconds:
+                    if copy[0] == colour:
+                        copy[1].wait_recv()
                 self.add(colour, 2, pos[(colour + 2) % 3], None, rb2, (0, 1))
-
-        def direct(self, phase):
+                self.direct(1, colour)
+
+        def points(self):
+            lines, self.last = self.last, []
+            for colour in (2, 1, 0):
+                self.settle(1, colour, lines)
+                self.direct(0, colour)
+
+        def finish(self):
+            for colour in (2, 1, 0):
+                self.settle(0, colour, self.last)
+
+        def direct(self, phase, colour):
             ref = r1 if phase == 1 else r0
-            self.last = []
             for n, off in ((2, 2), (0, 1), (1, -1)):
-                for colour in range(3):
-                    at = step((colour + phase) % 3, off)
-                    self.last.append(self.send(phase, colour, n, piece(self.wave, colour, phase, at, None, BACK),
-                                               self.land(ref, colour, phase, n, None), off))
-
-        def settle(self, phase):
+                at = step((colour + phase) % 3, off)
+                self.last.append((colour, self.send(
+                    phase, colour, n, piece(self.wave, colour, phase, at, None, BACK),
+                    self.land(ref, colour, phase, n, None), off)))
+
+        def settle(self, phase, colour, copies):
+            for which, copy in copies:
+                if which == colour:
+                    copy.wait_recv()
             ref = r1 if phase == 1 else r0
-            for copy in self.last:
-                copy.wait_recv()
-            for colour in range(3):
-                self.add(colour, phase, pos[(colour + phase) % 3], None, ref, (0, 1, 2))
+            self.add(colour, phase, pos[(colour + phase) % 3], None, ref, (0, 1, 2))
 
         def drain(self):
             for copy in self.all:
@@ -353,11 +368,11 @@
     picked0.append(pick(0, 1))
     loads[0].wait()
     loads[1].wait()
-    picked0[0].wait()
-    up_projection(0, 0, slots // 2)
+    up_projection(0, my_start, True)
+    for copy in picked0:
+        copy.wait()
     g1.relay()
-    picked0[1].wait()
-    up_projection(0, slots // 2, slots // 2)
+    up_projection(0, twin_start, False)
     activate()
     loads[2].wait()
     sent0 = [down_twin(0, 0), down_twin(0, 1)]
@@ -371,31 +386,27 @@
         s0.planes(colour)
     g1.arrive()
     picked1 = [pick(1, 0), pick(1, 1)]
-    picked1[0].wait()
-    up_projection(1, 0, slots // 2)
+    up_projection(1, my_start, True)
+    for copy in picked1:
+        copy.wait()
     s0.relay()
-    picked1[1].wait()
-    up_projection(1, slots // 2, slots // 2)
+    up_projection(1, twin_start, False)
     activate()
     sent1 = [down_twin(1, 0), down_twin(1, 1)]
     down_mine(1)
-    s0.own_plane()
-    s0.direct(1)
+    s0.lines()
     g1.drain()
     for copy in sent1:
         copy.wait()
     for colour in range(3):
         mix(1, colour)
         s1.planes(colour)
-    s0.settle(1)
-    s0.direct(0)
     s1.relay()
-    s0.settle(0)
-    s1.own_plane()
-    s1.direct(1)
-    s1.settle(1)
-    s1.direct(0)
-    s1.settle(0)
+    s0.points()
+    s1.lines()
+    s0.finish()
+    s1.points()
+    s1.finish()
     swap.wait_send()
     swap_facts.wait_send()
     ending = send(rows.at[1 - core, pos[0], pos[1], pos[2], :, body], final, swap_send, swap_recv, 1, twin)

time: 118 us -> 114 us (0.966)
  Pallas kernels: 115 us -> 111 us
    pallas_call x1, Pallas kernels: 115 us -> 111 us  [shards(): pl.pallas_call(kernel, out_shape=jax.ShapeDtypeStruct((tok, width), BF16)...]
where the time goes in v5:
time: 114 us; the launch traced here: 113 us
  Pallas kernels  111 us (97%)
  local copies, waits for them, and re-layouts  1.57 us (1%)
    pallas_call x1, Pallas kernels, shards(): pl.pallas_call(kernel, out_shape=jax.ShapeDtypeStruct((tok, width), BF16)...  111 us

profile of v5, /device:TPU:0, one launch (start us, length us, event | category | flops | bytes accessed | tf_op | source)
XLA Modules:
  0.0 112.9 jit_solution(18017151840385394659)
XLA Ops:
  0.0 111.3 %shard_map.64 = bf16[16,4096]{1,0:T(8,128)(2,1)} custom-call(bf16[16,4096]{1,0:T(8,128)(2,1)} %x_ref.1, s32[2,16]{1,0:T(2,128)} %bitcast.9, bf16[8,4096]{1,0:T(8,128)(2,1)} %bitcast.8, bf16[4096,896]{1,0:T(8,128)(2,1)} %bitcast.5, bf16[4096,896]{1,0:T(8,128)(2,1)} %bitcast.6, bf16[896,4096]{1,0:T(8,128)(2,1)} %bitcast.7), custom_call_target="tpu_custom_call" | custom-call | flops 22548578304 | bytes 22020096 | tf_op jit(solution)/shard_map/pallas_call | solution.py:428
  111.3 1.6 %copy.8 = bf16[16,4096]{1,0:T(8,128)(2,1)} copy(bf16[16,4096]{1,0:T(8,128)(2,1)} %shard_map.64) | data formatting | bytes 262144

commit v6 on v5

--- a/solution.py
+++ b/solution.py
@@ -117,32 +117,38 @@
             self.all.append(copy)
             return copy
 
-        def arrive(self):
-            for copy in self.last:
-                copy.wait_recv()
+        def arrive(self, only=None):
+            for colour, copy in self.last:
+                if only is None or colour == only:
+                    copy.wait_recv()
 
         def direct(self, phase):
-            self.arrive()
-            self.last = []
-            for n, off in enumerate(OFFSETS):
-                for colour in range(3):
+            now = []
+            for colour in range(3):
+                self.arrive(colour)
+                for n, off in ((2, 2), (0, 1), (1, -1)):
                     view = piece(self.wave, colour, phase, pos[(colour + phase) % 3], None, FORTH)
-                    self.last.append(self.send(phase, colour, n, view, off))
+                    now.append((colour, self.send(phase, colour, n, view, off)))
+            self.last = now
 
         def planes(self):
-            self.arrive()
-            self.last, self.relayed = [], []
-            for n, (off, half) in enumerate(((1, 0), (-1, 1), (1, 1), (-1, 0))):
-                for colour in range(3):
+            now, self.relayed = [], []
+            for colour in range(3):
+                self.arrive(colour)
+                for n, (off, half) in enumerate(((1, 0), (-1, 1), (1, 1), (-1, 0))):
                     view = piece(self.wave, colour, 2, pos[(colour + 2) % 3], half, FORTH)
                     copy = self.send(2, colour, n, view, off)
-                    (self.relayed if n < 2 else self.last).append((colour, off, half, copy) if n < 2 else copy)
+                    if n < 2:
+                        self.relayed.append((n, colour, off, half, copy))
+                    else:
+                        now.append((colour, copy))
+            self.last = now
 
         def relay(self):
-            for n, (colour, off, half, copy) in enumerate(self.relayed):
+            for n, colour, off, half, copy in self.relayed:
                 copy.wait_recv()
                 view = piece(self.wave, colour, 2, step((colour + 2) % 3, -off), half, FORTH)
-                self.last.append(self.send(2, colour, 4 + n // 3, view, off))
+                self.last.append((colour, self.send(2, colour, 4 + n, view, off)))
 
         def drain(self):
             for copy in self.all:
@@ -167,7 +173,7 @@
     wide_f = wide.astype(F32)
 
     def placing(wave, g):
-        facts = rows[wave, lax.div(g, 2), pl.ds(lax.rem(g, 2) * 2, 2), :, :, tail].reshape(LANES, LANES).astype(F32)
+        facts = rows[wave, g // 2, pl.ds(g % 2 * 2, 2), :, :, tail].reshape(LANES, LANES).astype(F32)
         plain = jnp.zeros((LANES, LANES), F32)
         weighted = jnp.zeros((LANES, LANES), F32)
         for which, base in ((expert, 0.0), (other_expert, float(span))):
@@ -188,16 +194,17 @@
     def pick(wave, part):
         def one(g, carry):
             place = placing(wave, g)
-            at = pl.ds(pl.multiple_of(g * span, span), span)
+            at = pl.ds(g * span, span)
             for n in range(half_width // chunk):
-                block = rows[wave, lax.div(g, 2), pl.ds(lax.rem(g, 2) * 2, 2), :, :, pl.ds(n * chunk, chunk)]
+                block = rows[wave, g // 2, pl.ds(g % 2 * 2, 2), :, :, pl.ds(n * chunk, chunk)]
                 got = lax.dot_general(place, block.reshape(LANES, chunk), (((0,), (0,)), ((), ())),
                                       preferred_element_type=F32).astype(BF16)
                 xs[wave, at, pl.ds(pl.multiple_of(my_start + n * chunk, chunk), chunk)] = got[:span]
                 staging[at, pl.ds(n * chunk, chunk)] = got[span:]
             return carry
 
-        lax.fori_loop(part * 4, part * 4 + 4, one, 0)
+        for g in range(part * 4, part * 4 + 4):
+            one(g, 0)
         at = pl.ds(part * 256, 256)
         return send(staging.at[at], xs.at[wave, at, pl.ds(my_start, half_width)],
                     in_send, in_recv, wave * 2 + part, twin)

time: 114 us -> 111 us (0.974)
  Pallas kernels: 111 us -> 108 us
    pallas_call x1, Pallas kernels: 111 us -> 108 us  [shards(): pl.pallas_call(kernel, out_shape=jax.ShapeDtypeStruct((tok, width), BF16)...]
where the time goes in v6:
time: 111 us; the launch traced here: 110 us
  Pallas kernels  108 us (97%)
  local copies, waits for them, and re-layouts  1.57 us (1%)
    pallas_call x1, Pallas kernels, shards(): pl.pallas_call(kernel, out_shape=jax.ShapeDtypeStruct((tok, width), BF16)...  108 us

profile of v6, /device:TPU:0, one launch (start us, length us, event | category | flops | bytes accessed | tf_op | source)
XLA Modules:
  0.0 109.7 jit_solution(15543844183976332980)
XLA Ops:
  0.0 108.1 %shard_map.64 = bf16[16,4096]{1,0:T(8,128)(2,1)} custom-call(bf16[16,4096]{1,0:T(8,128)(2,1)} %x_ref.1, s32[2,16]{1,0:T(2,128)} %bitcast.9, bf16[8,4096]{1,0:T(8,128)(2,1)} %bitcast.8, bf16[4096,896]{1,0:T(8,128)(2,1)} %bitcast.5, bf16[4096,896]{1,0:T(8,128)(2,1)} %bitcast.6, bf16[896,4096]{1,0:T(8,128)(2,1)} %bitcast.7), custom_call_target="tpu_custom_call" | custom-call | flops 22548578304 | bytes 22020096 | tf_op jit(solution)/shard_map/pallas_call | solution.py:435
  108.1 1.6 %copy.8 = bf16[16,4096]{1,0:T(8,128)(2,1)} copy(bf16[16,4096]{1,0:T(8,128)(2,1)} %shard_map.64) | data formatting | bytes 262144
